TPU v7x, 32 devices: a whole 2x2x4 slice. The times are simulated.
32 devices in a mesh: rep: 2 (over y), tp: 16 (over z, x, core).
Axes of the slice: x: 2, y: 2, z: 4, core: 2. Of those that a mesh axis runs over, the one named last changes fastest.
Arguments:
- queries: bfloat16 [4096, 16384], P(('rep', 'tp')), parts along dimension 0, may hold values from -120 to 120
- keyvals: bfloat16 [4096, 2048], P(('rep', 'tp')), parts along dimension 0, may hold values from -6 to 6
- parent: int32 [32], P('rep'), parts along dimension 0, may hold values from -1 to 13, as said below
- counts: int32 [32], P('rep'), parts along dimension 0, may hold values from 32 to 128
Outputs:
- attended: bfloat16 [4096, 16384], P(('rep', 'tp')), parts along dimension 0
There are 2 independent parts, one for each index of `rep`. A program takes and returns all parts, laid end to end along the dimension named above; each array names one. Nothing has to cross between parts.
Inputs may be any that keep to these rules, and one draw needn't show every extreme that they name: Segments whose numbers agree modulo 16 // 8 form one tree of 8 segments; the lowest of a tree has parent -1, every other one a parent with a lower number in its tree. In every draw some segment has 7 ancestors.
All inputs are finite; a program needn't handle non-finite values.
Results may differ from a plain program's by a relative error of at most 0.004.
Values may be sent and summed in bfloat16 or wider, within the bound.
No kernel may reach another device: no remote copies, remote signals or barrier semaphores. Data moves between devices by JAX's collectives and lax.ppermute only.
A program may use at most 128 MiB of HBM per device.

v0:
```python
from functools import partial

import jax
import jax.numpy as jnp
from jax import lax
from jax.experimental import pallas as pl
from jax.experimental.pallas import tpu as pltpu
from jax.sharding import PartitionSpec as P

HD = 128
SPAN = 8
TILE = 32
NEG = -1e30
SCALE = HD ** (-0.5)
FACTOR = SCALE * 1.4426950408889634
SMALLEST, LARGEST = 2.0 ** -60, 2.0 ** 100
STATE = HD + 8
VROWS = HD + 16
TOTAL, SHIFT = HD, HD + 1
UNIT = 4
STEP = 2
VMEM = 20 * 1024 * 1024


def parent_of(table_ref, segment):
    return table_ref[1 + segment]


def count_of(table_ref, segment):
    return table_ref[1 + (table_ref.shape[0] - 1) // 2 + segment]


def is_ancestor(table_ref, me, source):
    current = me
    hit = jnp.int32(0)
    for _ in range(SPAN - 1):
        current = jnp.where(current >= 0, parent_of(table_ref, jnp.maximum(current, 0)), -1)
        hit = jnp.where(current == source, 1, hit)
    return jnp.where(source >= 0, hit, 0)


def source_of(me, stride, shift, swap):
    offset = me // stride
    base = offset
    if swap:
        base = jnp.where(offset % 2 == 0, offset + 1, offset - 1)
    base = base - shift
    return jnp.where(base >= 0, base * stride + me % stride, -1)


def live_keys(table_ref, me, stride, move):
    if move is None:
        return count_of(table_ref, me)
    source = source_of(me, stride, *move)
    length = count_of(table_ref, jnp.maximum(source, 0))
    return jnp.where(is_ancestor(table_ref, me, source) > 0, length, 0)


def attend(stride, moves, blocks, parts, first, last, table_ref, *refs):
    refs = list(refs)
    n, many = len(moves), len(parts)
    if first:
        q_ref = refs.pop(0)
    else:
        qt_refs = [refs.pop(0) for _ in parts]
        old_refs = [refs.pop(0) for _ in parts]
    kv_refs = [[refs.pop(0) for _ in moves] for _ in parts]
    if last:
        out_ref = refs.pop(0)
    else:
        if first:
            qt_refs = [refs.pop(0) for _ in parts]
        new_refs = [refs.pop(0) for _ in parts]
    k_buf, v_buf, bad_buf = refs

    me = table_ref[0]
    count = count_of(table_ref, me)
    held, _, across_all = qt_refs[0].shape
    rows = v_buf.shape[2] // n
    tiles_max = rows // TILE
    lanes = across_all // tiles_max
    group = lanes // TILE
    tiles = (count + TILE - 1) // TILE
    steps = held // STEP
    head = (pl.program_id(0) % steps) * STEP
    turn_of = pl.program_id(0) // steps
    lengths = [live_keys(table_ref, me, stride, m) for m in moves]

    j_lanes = lax.broadcasted_iota(jnp.int32, (VROWS - HD, rows), 1)
    sub = lax.broadcasted_iota(jnp.int32, (VROWS - HD, rows), 0)

    def fill(i):
        for l in range(n):
            to = slice(l * rows, (l + 1) * rows)
            of = slice(blocks[i][l] * rows, (blocks[i][l] + 1) * rows)
            inside = jnp.where(j_lanes < lengths[l], 1.0, 0.0)
            for h in range(STEP):
                base = pl.multiple_of((head + h) * 2 * HD, 2 * HD)
                k_buf[h, to, :] = kv_refs[i][l][of, pl.ds(base, HD)]
                value = kv_refs[i][l][of, pl.ds(base + HD, HD)]
                v_buf[h, :HD, to] = value.T * inside[:1].astype(jnp.bfloat16)
                v_buf[h, HD:, to] = jnp.where(sub == 0, inside, 0.0).astype(jnp.bfloat16)

    def across(t, k=1):
        if isinstance(t, int):
            return slice(t * lanes, (t + k) * lanes)
        return pl.ds(pl.multiple_of(t * lanes, lanes), k * lanes)

    def down(t):
        if isinstance(t, int):
            return slice(t * TILE, (t + 1) * TILE)
        return pl.ds(pl.multiple_of(t * TILE, TILE), TILE)

    def causal(t, width):
        j = lax.broadcasted_iota(jnp.int32, (rows, width), 0)
        lane = lax.broadcasted_iota(jnp.int32, (rows, width), 1)
        return j <= lane % TILE + (lane // lanes + t) * TILE

    def turned(i, h, t, k):
        if first:
            base = (parts[i] * held + head + h) * group * HD
            for u in range(k):
                heads = [
                    q_ref[down(t + u), pl.ds(pl.multiple_of(base + g * HD, HD), HD)] for g in range(group)
                ]
                qt_refs[i][head + h, :, across(t + u)] = jnp.concatenate(heads, axis=0).T
        return qt_refs[i][head + h, :, across(t, k)]

    def scores(i, h, t, k):
        return jnp.dot(k_buf[h], turned(i, h, t, k), preferred_element_type=jnp.float32)

    def mix(h, weights):
        return jnp.dot(v_buf[h], weights, preferred_element_type=jnp.float32)[:STATE]

    def finish(i, h, t, k, mixed, shift):
        if last:
            result = (mixed[:HD] * (1.0 / mixed[TOTAL:TOTAL + 1])).astype(out_ref.dtype).T
            for u in range(k):
                base = (t + u) * TILE
                live = lax.broadcasted_iota(jnp.int32, (TILE, HD), 0) + base < count
                for g in range(group):
                    at = u * lanes + g * TILE
                    piece = jnp.where(live, result[at:at + TILE].astype(jnp.float32), 0.0)
                    to = (h * group + g) * HD
                    out_ref[down(t + u), to:to + HD] = piece.astype(out_ref.dtype)
        else:
            new_refs[i][head + h, :, across(t, k)] = mixed
            new_refs[i][head + h, SHIFT:SHIFT + 1, across(t, k)] = shift

    def unshifted(i, h, t, k, s):
        w = jnp.exp2(s * FACTOR)
        if first:
            own = jnp.where(causal(t, k * lanes), w[:rows], 0.0)
            w = jnp.concatenate([own, w[rows:]], axis=0) if n > 1 else own
        mixed = mix(h, w.astype(jnp.bfloat16))
        if not first:
            mixed = mixed + old_refs[i][head + h, :, across(t, k)]
        total = mixed[TOTAL:TOTAL + 1]
        good = (total >= SMALLEST) & (total <= LARGEST)
        if not first:
            good = good & (old_refs[i][head + h, SHIFT:SHIFT + 1, across(t, k)] == 0.0)
        bad_buf[h:h + 1, across(t, k)] = jnp.where(good, 0.0, 1.0)
        finish(i, h, t, k, mixed, jnp.zeros((1, k * lanes), jnp.float32))

    def shifted(i, h, t, _):
        s = scores(i, h, t, 1)
        pieces = []
        for l in range(n):
            j = lax.broadcasted_iota(jnp.int32, (rows, lanes), 0)
            allowed = j < lengths[l]
            if moves[l] is None:
                allowed = allowed & causal(t, lanes)
            pieces.append(jnp.where(allowed, s[l * rows:(l + 1) * rows], NEG))
        s = jnp.concatenate(pieces, axis=0)
        top = jnp.max(s, axis=0, keepdims=True)
        if not first:
            before = old_refs[i][head + h, SHIFT:SHIFT + 1, across(t)]
            top = jnp.maximum(top, before)
        w = jnp.exp2((s - top) * FACTOR)
        mixed = mix(h, w.astype(jnp.bfloat16))
        if not first:
            mixed = mixed + old_refs[i][head + h, :, across(t)] * jnp.exp2((before - top) * FACTOR)
        finish(i, h, t, 1, mixed, top)
        return 0

    def run(i, k):
        units = [(i, h, t, min(UNIT, k - t)) for h in range(STEP) for t in range(0, k, UNIT)]
        s = scores(*units[0])
        for at, unit in enumerate(units):
            following = scores(*units[at + 1]) if at + 1 < len(units) else None
            unshifted(*unit, s)
            s = following

    def safely(i):
        for h in range(STEP):
            lax.fori_loop(0, tiles, partial(shifted, i, h), 0)

    def mine(i):
        return turn_of == i if many > 1 else turn_of >= 0

    bad_buf[...] = jnp.zeros(bad_buf.shape, jnp.float32)
    for i in range(many):
        pl.when(mine(i))(partial(fill, i))
    some = sum(lengths) > 0
    for i in range(many):
        for k in range(1, tiles_max + 1):
            pl.when(mine(i) & (tiles == k) & (some | last))(partial(run, i, k))

    def keep(i):
        for h in range(STEP):
            new_refs[i][head + h] = old_refs[i][head + h]

    if not (first or last):
        for i in range(many):
            pl.when(mine(i) & jnp.logical_not(some))(partial(keep, i))
    bad = jnp.max(bad_buf[:STEP, :]) > 0.0
    for i in range(many):
        pl.when(mine(i) & bad)(partial(safely, i))

    if last:
        def clear(t, _):
            out_ref[down(t), :] = jnp.zeros((TILE, out_ref.shape[1]), out_ref.dtype)
            return 0

        lax.fori_loop(tiles, tiles_max, clear, 0)


def levels(stride, table, queries, kv_heads, moves, kvs, state, parts=(0, 1), last=False):
    rows, width = queries.shape
    group = width // HD // kv_heads
    half = kv_heads // 2
    tiles_max = rows // TILE
    lanes = group * TILE
    first = state is None
    steps = half // STEP
    n = len(moves)
    whole = pl.BlockSpec(memory_space=pltpu.VMEM)
    if first:
        operands = [queries]
    else:
        operands = [state[part][0] for part in parts] + [state[part][1] for part in parts]
    operands += [array for part in parts for array, _ in kvs[part]]
    if last:
        out_specs = pl.BlockSpec((rows, STEP * group * HD), lambda k, *_: (0, k))
        out_shape = jax.ShapeDtypeStruct((rows, width), jnp.bfloat16)
    else:
        turned = jax.ShapeDtypeStruct((half, HD, tiles_max * lanes), jnp.bfloat16)
        held = jax.ShapeDtypeStruct((half, STATE, tiles_max * lanes), jnp.float32)
        out_shape = [turned] * (len(parts) if first else 0) + [held] * len(parts)
        out_specs = [whole] * len(out_shape)
    result = pl.pallas_call(
        partial(attend, stride, moves, [[block for _, block in kvs[part]] for part in parts], parts, first, last),
        grid_spec=pltpu.PrefetchScalarGridSpec(
            num_scalar_prefetch=1,
            grid=(len(parts) * steps,),
            in_specs=[whole] * len(operands),
            out_specs=out_specs,
            scratch_shapes=[
                pltpu.VMEM((STEP, n * rows, HD), jnp.bfloat16),
                pltpu.VMEM((STEP, VROWS, n * rows), jnp.bfloat16),
                pltpu.VMEM((8, tiles_max * lanes), jnp.float32),
            ],
        ),
        out_shape=out_shape,
        compiler_params=pltpu.CompilerParams(vmem_limit_bytes=VMEM),
        cost_estimate=pl.CostEstimate(
            flops=2 * rows * rows * width * n * len(parts),
            bytes_accessed=rows * width * len(parts),
            transcendentals=rows * rows * width // HD * n // 2 * len(parts),
        ),
        name="levels_" + str(n) + ("_first" if first else "_last" if last else ""),
    )(table, *operands)
    if last:
        return result
    state = {} if first else dict(state)
    for at, part in enumerate(parts):
        state[part] = (result[at], result[len(parts) + at]) if first else (state[part][0], result[at])
    return state


def per_device(queries, keyvals, parent, counts):
    rows, width = queries.shape
    kv_heads = keyvals.shape[1] // (2 * HD)
    half = kv_heads // 2
    segments = lax.axis_size("tp")
    stride = segments // SPAN
    me = lax.axis_index("tp").reshape(1).astype(jnp.int32)
    table = jnp.concatenate([me, parent, counts])

    def send(x, pairs):
        full = [(a * stride + t, b * stride + t) for a, b in pairs for t in range(stride)]
        return lax.ppermute(x, "tp", full)

    def kernel(moves, kvs, state, **more):
        return levels(stride, table, queries, kv_heads, moves, kvs, state, **more)

    def halves(*arrays):
        return [[(array, part) for array in arrays] for part in (0, 1)]

    swap = [(o, o ^ 1) for o in range(SPAN)]
    up = [(o, (o + 2) % SPAN) for o in range(SPAN)]
    cut = half * 2 * HD
    hold = lax.optimization_barrier
    m1 = [(2, False), (0, True)]
    m2 = [(4, False), (2, True)]
    m3 = [(6, False), (4, True)]
    m4 = [(6, True)]
    both = jnp.concatenate([keyvals[:, :cut], keyvals[:, cut:]], axis=0)
    z1, x1 = send(both, up), send(both, swap)
    state = kernel([None], halves(both), None)
    z1, x1, state = hold((z1, x1, state))
    az1, bz1 = z1[:rows], z1[rows:]
    az2, ax2 = send(az1, up), send(az1, swap)
    bz2, bx2 = send(bz1, up), send(bz1, swap)
    state = kernel(m1, halves(z1, x1), state)
    az2, ax2, state = hold((az2, ax2, state))
    az3, ax3 = send(az2, [(o, o + 2) for o in range(4, SPAN - 2)]), send(az2, swap)
    state = kernel(m2, [[(az2, 0), (ax2, 0)], None], state, parts=(0,))
    bz2, bx2, state = hold((bz2, bx2, state))
    bz3, bx3 = send(bz2, [(o, o + 2) for o in range(4, SPAN - 2)]), send(bz2, swap)
    state = kernel(m2, [None, [(bz2, 0), (bx2, 0)]], state, parts=(1,))
    az3, ax3, state = hold((az3, ax3, state))
    a4 = send(az3, swap)
    state = kernel(m3, [[(az3, 0), (ax3, 0)], None], state, parts=(0,))
    bz3, bx3, state = hold((bz3, bx3, state))
    b4 = send(bx3, [(o, o + 2) for o in range(4, SPAN - 2)])
    state = kernel(m3, [None, [(bz3, 0), (bx3, 0)]], state, parts=(1,))
    a4, b4, state = hold((a4, b4, state))
    return kernel(m4, [[(a4, 0)], [(b4, 0)]], state, last=True)

def solution(mesh):
    in_specs = (P(("rep", "tp"), None), P(("rep", "tp"), None), P("rep"), P("rep"))
    out_specs = P(("rep", "tp"), None)
    return jax.shard_map(
        per_device, mesh=mesh, in_specs=in_specs, out_specs=out_specs, check_vma=False
    )
```

profile of v0, /device:TPU:24, one launch (start us, length us, event | category | flops | bytes accessed | tf_op | source)
XLA Modules:
  0.0 123.4 jit_solution(7446681550382705669)
XLA Ops:
  0.0 1.1 fusion.1
  1.1 1.6 %collective-permute-start.1 = (bf16[256,1024]{1,0:T(8,128)(2,1)S(1)}, bf16[256,1024]{1,0:T(8,128)(2,1)S(1)}, u32[]{:S(2)}, u32[]{:S(2)}) collective-permute-start(bf16[256,1024]{1,0:T(8,128)(2,1)S(1)} %pad_maximum_fusion.refs_1_.refs_2_), channel_id=1, source_target_pairs={{0,2},{1,3},{2,0},{3,1},{4,6},{5,7},{6,4},{7,5},{8,10},{9,11},{10,... | collective-permute-start | bytes 1572872 | tf_op jit(solution)/shard_map/ppermute | solution.py:292
  2.7 0.2 collective-permute-start
  2.9 0.7 pad_add_fusion.table_ref
  3.6 2.2 %copy-done = bf16[128,16384]{1,0:T(8,128)(2,1)S(1)} copy-done((bf16[128,16384]{1,0:T(8,128)(2,1)S(1)}, bf16[128,16384]{1,0:T(8,128)(2,1)}, u32[]{:S(2)}) %copy-start) | copy-done | bytes 4194328
  5.8 19.6 %levels_1_first.1 = (bf16[4,128,2048]{2,1,0:T(8,128)(2,1)S(1)}, bf16[4,128,2048]{2,1,0:T(8,128)(2,1)S(1)}, f32[4,136,2048]{2,1,0:T(8,128)S(1)}, f32[4,136,2048]{2,1,0:T(8,128)S(1)}) custom-call(s32[33]{0:T(128)S(1)} %pad_add_fusion.table_ref, bf16[128,16384]{1,0:T(8,128)(2,1)S(1)} %copy-done, bf16[256,1024]{1,0:T(8,128)(2,1)S(1)} %pad_maximum_fusion.refs_1_.refs_2_, ...), custom_call_target="tpu_custom_call" | custom-call | flops 1073741824 | bytes 4194304 | tf_op jit(solution)/shard_map/levels_1_first/pallas_call | solution.py:251
  25.4 0.0 collective-permute-done.refs_4_.refs_6_
  25.5 0.4 collective-permute-start.3
  25.9 0.0 collective-permute-start.2
  25.9 1.7 %collective-permute-start.7 = (bf16[128,1024]{1,0:T(8,128)(2,1)S(1)}, bf16[128,1024]{1,0:T(8,128)(2,1)S(1)}, u32[]{:S(2)}, u32[]{:S(2)}) collective-permute-start(bf16[128,1024]{1,0:T(8,128)(2,1)S(1)} %get-tuple-element.89), channel_id=1, source_target_pairs={{0,2},{1,3},{2,0},{3,1},{4,6},{5,7},{6,4},{7,5},{8,10},{9,11},{10,... | collective-permute-start | bytes 786440 | tf_op jit(solution)/shard_map/ppermute | solution.py:292
  27.6 3.2 %collective-permute-start.6 = (bf16[128,1024]{1,0:T(8,128)(2,1)S(1)}, bf16[128,1024]{1,0:T(8,128)(2,1)S(1)}, u32[]{:S(2)}, u32[]{:S(2)}) collective-permute-start(bf16[128,1024]{1,0:T(8,128)(2,1)S(1)} %get-tuple-element.89), channel_id=1, source_target_pairs={{0,4},{1,5},{2,6},{3,7},{4,8},{5,9},{6,10},{7,11},{8,12},{9,13},{1... | collective-permute-start | bytes 786440 | tf_op jit(solution)/shard_map/ppermute | solution.py:292
  30.7 21.5 %levels_2.5 = (f32[4,136,2048]{2,1,0:T(8,128)S(1)}, f32[4,136,2048]{2,1,0:T(8,128)S(1)}) custom-call(s32[33]{0:T(128)S(1)} %pad_add_fusion.table_ref, bf16[4,128,2048]{2,1,0:T(8,128)(2,1)S(1)} %get-tuple-element.83.refs_0_, bf16[4,128,2048]{2,1,0:T(8,128)(2,1)S(1)} %get-tuple-element.84.refs_1_.refs_0_, f32[4,136,2048]{2,1,0:T(8,128)S(1)} %get-tuple-element.54.refs_2_, ...), custom_call_target="tpu_custom_call" | custom-call | flops 2147483648 | bytes 4194304 | tf_op jit(solution)/shard_map/levels_2/pallas_call | solution.py:251
  52.2 0.0 collective-permute-done.2.refs_2_
  52.3 0.1 collective-permute-start.5
  52.3 1.3 %collective-permute-start.4 = (bf16[128,1024]{1,0:T(8,128)(2,1)S(1)}, bf16[128,1024]{1,0:T(8,128)(2,1)S(1)}, u32[]{:S(2)}, u32[]{:S(2)}) collective-permute-start(bf16[128,1024]{1,0:T(8,128)(2,1)S(1)} %collective-permute-done.2.refs_2_), channel_id=1, source_target_pairs={{8,12},{9,13},{10,14},{11,15},{24,28},{25,29},{26,30},{27,31}} | collective-permute-start | bytes 786440 | tf_op jit(solution)/shard_map/ppermute | solution.py:292
  53.6 11.0 %levels_2.6.refs_1_ = f32[4,136,2048]{2,1,0:T(8,128)S(1)} custom-call(s32[33]{0:T(128)S(1)} %pad_add_fusion.table_ref, bf16[4,128,2048]{2,1,0:T(8,128)(2,1)S(1)} %get-tuple-element.83.refs_0_, f32[4,136,2048]{2,1,0:T(8,128)S(1)} %get-tuple-element.61.refs_1_, bf16[128,1024]{1,0:T(8,128)(2,1)S(1)} %collective-permute-done.2.refs_2_, ...), custom_call_target="tpu_custom_call" | custom-call | flops 1073741824 | bytes 2097152 | tf_op jit(solution)/shard_map/levels_2/pallas_call | solution.py:251
  64.7 0.1 collective-permute-start.10
  64.7 1.5 %collective-permute-start.9 = (bf16[128,1024]{1,0:T(8,128)(2,1)S(1)}, bf16[128,1024]{1,0:T(8,128)(2,1)S(1)}, u32[]{:S(2)}, u32[]{:S(2)}) collective-permute-start(bf16[128,1024]{1,0:T(8,128)(2,1)S(1)} %collective-permute-done.6.refs_2_), channel_id=1, source_target_pairs={{8,12},{9,13},{10,14},{11,15},{24,28},{25,29},{26,30},{27,31}} | collective-permute-start | bytes 786440 | tf_op jit(solution)/shard_map/ppermute | solution.py:292
  66.3 10.9 %levels_2.7.refs_1_ = f32[4,136,2048]{2,1,0:T(8,128)S(1)} custom-call(s32[33]{0:T(128)S(1)} %pad_add_fusion.table_ref, bf16[4,128,2048]{2,1,0:T(8,128)(2,1)S(1)} %get-tuple-element.84.refs_1_.refs_0_, f32[4,136,2048]{2,1,0:T(8,128)S(1)} %get-tuple-element.68.refs_1_, bf16[128,1024]{1,0:T(8,128)(2,1)S(1)} %collective-permute-done.6.refs_2_, ...), custom_call_target="tpu_custom_call" | custom-call | flops 1073741824 | bytes 2097152 | tf_op jit(solution)/shard_map/levels_2/pallas_call | solution.py:251
  77.2 10.9 %levels_2.8.refs_2_ = f32[4,136,2048]{2,1,0:T(8,128)S(1)} custom-call(s32[33]{0:T(128)S(1)} %pad_add_fusion.table_ref, bf16[4,128,2048]{2,1,0:T(8,128)(2,1)S(1)} %get-tuple-element.83.refs_0_, f32[4,136,2048]{2,1,0:T(8,128)S(1)} %levels_2.6.refs_1_, bf16[128,1024]{1,0:T(8,128)(2,1)S(1)} %collective-permute-done.4.refs_2_, ...), custom_call_target="tpu_custom_call" | custom-call | flops 1073741824 | bytes 2097152 | tf_op jit(solution)/shard_map/levels_2/pallas_call | solution.py:251
  88.2 1.6 %collective-permute-start.11 = (bf16[128,1024]{1,0:T(8,128)(2,1)S(1)}, bf16[128,1024]{1,0:T(8,128)(2,1)S(1)}, u32[]{:S(2)}, u32[]{:S(2)}) collective-permute-start(bf16[128,1024]{1,0:T(8,128)(2,1)S(1)} %collective-permute-done.10.refs_3_), channel_id=1, source_target_pairs={{8,12},{9,13},{10,14},{11,15},{24,28},{25,29},{26,30},{27,31}} | collective-permute-start | bytes 786440 | tf_op jit(solution)/shard_map/ppermute | solution.py:292
  89.7 0.1 collective-permute-start.8
  89.8 10.9 %levels_2.9.refs_3_ = f32[4,136,2048]{2,1,0:T(8,128)S(1)} custom-call(s32[33]{0:T(128)S(1)} %pad_add_fusion.table_ref, bf16[4,128,2048]{2,1,0:T(8,128)(2,1)S(1)} %get-tuple-element.84.refs_1_.refs_0_, f32[4,136,2048]{2,1,0:T(8,128)S(1)} %levels_2.7.refs_1_, bf16[128,1024]{1,0:T(8,128)(2,1)S(1)} %collective-permute-done.9.refs_2_, ...), custom_call_target="tpu_custom_call" | custom-call | flops 1073741824 | bytes 2097152 | tf_op jit(solution)/shard_map/levels_2/pallas_call | solution.py:251
  100.8 22.7 %levels_1_last.1 = bf16[128,16384]{1,0:T(8,128)(2,1)} custom-call(s32[33]{0:T(128)S(1)} %pad_add_fusion.table_ref, bf16[4,128,2048]{2,1,0:T(8,128)(2,1)S(1)} %get-tuple-element.83.refs_0_, bf16[4,128,2048]{2,1,0:T(8,128)(2,1)S(1)} %get-tuple-element.84.refs_1_.refs_0_, f32[4,136,2048]{2,1,0:T(8,128)S(1)} %levels_2.8.refs_2_, ...), custom_call_target="tpu_custom_call" | custom-call | flops 1073741824 | bytes 4194304 | tf_op jit(solution)/shard_map/levels_1_last/pallas_call | solution.py:251
  (13 shorter events, 0.1 us)
Async XLA Ops:
  1.1 24.3 %collective-permute-start.1 = (bf16[256,1024]{1,0:T(8,128)(2,1)S(1)}, bf16[256,1024]{1,0:T(8,128)(2,1)S(1)}, u32[]{:S(2)}, u32[]{:S(2)}) collective-permute-start(bf16[256,1024]{1,0:T(8,128)(2,1)S(1)} %pad_maximum_fusion.refs_1_.refs_2_), channel_id=1, source_target_pairs={{0,2},{1,3},{2,0},{3,1},{4,6},{5,7},{6,4},{7,5},{8,10},{9,11},{10,... | collective-permute-start | bytes 1572872 | tf_op jit(solution)/shard_map/ppermute | solution.py:292
  2.7 22.8 %collective-permute-start = (bf16[256,1024]{1,0:T(8,128)(2,1)S(1)}, bf16[256,1024]{1,0:T(8,128)(2,1)S(1)}, u32[]{:S(2)}, u32[]{:S(2)}) collective-permute-start(bf16[256,1024]{1,0:T(8,128)(2,1)S(1)} %pad_maximum_fusion.refs_1_.refs_2_), channel_id=1, source_target_pairs={{0,4},{1,5},{2,6},{3,7},{4,8},{5,9},{6,10},{7,11},{8,12},{9,13},{1... | collective-permute-start | bytes 1572872 | tf_op jit(solution)/shard_map/ppermute | solution.py:292
  3.6 2.2 %copy-start = (bf16[128,16384]{1,0:T(8,128)(2,1)S(1)}, bf16[128,16384]{1,0:T(8,128)(2,1)}, u32[]{:S(2)}) copy-start(bf16[128,16384]{1,0:T(8,128)(2,1)} %refs_0_.1) | copy-start | bytes 12582916
  25.5 26.8 %collective-permute-start.3 = (bf16[128,1024]{1,0:T(8,128)(2,1)S(1)}, bf16[128,1024]{1,0:T(8,128)(2,1)S(1)}, u32[]{:S(2)}, u32[]{:S(2)}) collective-permute-start(bf16[128,1024]{1,0:T(8,128)(2,1)S(1)} %get-tuple-element.90), channel_id=1, source_target_pairs={{0,2},{1,3},{2,0},{3,1},{4,6},{5,7},{6,4},{7,5},{8,10},{9,11},{10,... | collective-permute-start | bytes 786440 | tf_op jit(solution)/shard_map/ppermute | solution.py:292
  25.9 26.4 %collective-permute-start.2 = (bf16[128,1024]{1,0:T(8,128)(2,1)S(1)}, bf16[128,1024]{1,0:T(8,128)(2,1)S(1)}, u32[]{:S(2)}, u32[]{:S(2)}) collective-permute-start(bf16[128,1024]{1,0:T(8,128)(2,1)S(1)} %get-tuple-element.90), channel_id=1, source_target_pairs={{0,4},{1,5},{2,6},{3,7},{4,8},{5,9},{6,10},{7,11},{8,12},{9,13},{1... | collective-permute-start | bytes 786440 | tf_op jit(solution)/shard_map/ppermute | solution.py:292
  25.9 38.8 %collective-permute-start.7 = (bf16[128,1024]{1,0:T(8,128)(2,1)S(1)}, bf16[128,1024]{1,0:T(8,128)(2,1)S(1)}, u32[]{:S(2)}, u32[]{:S(2)}) collective-permute-start(bf16[128,1024]{1,0:T(8,128)(2,1)S(1)} %get-tuple-element.89), channel_id=1, source_target_pairs={{0,2},{1,3},{2,0},{3,1},{4,6},{5,7},{6,4},{7,5},{8,10},{9,11},{10,... | collective-permute-start | bytes 786440 | tf_op jit(solution)/shard_map/ppermute | solution.py:292
  27.6 37.1 %collective-permute-start.6 = (bf16[128,1024]{1,0:T(8,128)(2,1)S(1)}, bf16[128,1024]{1,0:T(8,128)(2,1)S(1)}, u32[]{:S(2)}, u32[]{:S(2)}) collective-permute-start(bf16[128,1024]{1,0:T(8,128)(2,1)S(1)} %get-tuple-element.89), channel_id=1, source_target_pairs={{0,4},{1,5},{2,6},{3,7},{4,8},{5,9},{6,10},{7,11},{8,12},{9,13},{1... | collective-permute-start | bytes 786440 | tf_op jit(solution)/shard_map/ppermute | solution.py:292
  52.3 24.9 %collective-permute-start.5 = (bf16[128,1024]{1,0:T(8,128)(2,1)S(1)}, bf16[128,1024]{1,0:T(8,128)(2,1)S(1)}, u32[]{:S(2)}, u32[]{:S(2)}) collective-permute-start(bf16[128,1024]{1,0:T(8,128)(2,1)S(1)} %collective-permute-done.2.refs_2_), channel_id=1, source_target_pairs={{0,2},{1,3},{2,0},{3,1},{4,6},{5,7},{6,4},{7,5},{8,10},{9,11},{10,... | collective-permute-start | bytes 786440 | tf_op jit(solution)/shard_map/ppermute | solution.py:292
  52.3 24.9 %collective-permute-start.4 = (bf16[128,1024]{1,0:T(8,128)(2,1)S(1)}, bf16[128,1024]{1,0:T(8,128)(2,1)S(1)}, u32[]{:S(2)}, u32[]{:S(2)}) collective-permute-start(bf16[128,1024]{1,0:T(8,128)(2,1)S(1)} %collective-permute-done.2.refs_2_), channel_id=1, source_target_pairs={{8,12},{9,13},{10,14},{11,15},{24,28},{25,29},{26,30},{27,31}} | collective-permute-start | bytes 786440 | tf_op jit(solution)/shard_map/ppermute | solution.py:292
  64.7 23.5 %collective-permute-start.10 = (bf16[128,1024]{1,0:T(8,128)(2,1)S(1)}, bf16[128,1024]{1,0:T(8,128)(2,1)S(1)}, u32[]{:S(2)}, u32[]{:S(2)}) collective-permute-start(bf16[128,1024]{1,0:T(8,128)(2,1)S(1)} %collective-permute-done.6.refs_2_), channel_id=1, source_target_pairs={{0,2},{1,3},{2,0},{3,1},{4,6},{5,7},{6,4},{7,5},{8,10},{9,11},{10,... | collective-permute-start | bytes 786440 | tf_op jit(solution)/shard_map/ppermute | solution.py:292
  64.7 23.4 %collective-permute-start.9 = (bf16[128,1024]{1,0:T(8,128)(2,1)S(1)}, bf16[128,1024]{1,0:T(8,128)(2,1)S(1)}, u32[]{:S(2)}, u32[]{:S(2)}) collective-permute-start(bf16[128,1024]{1,0:T(8,128)(2,1)S(1)} %collective-permute-done.6.refs_2_), channel_id=1, source_target_pairs={{8,12},{9,13},{10,14},{11,15},{24,28},{25,29},{26,30},{27,31}} | collective-permute-start | bytes 786440 | tf_op jit(solution)/shard_map/ppermute | solution.py:292
  88.2 12.6 %collective-permute-start.11 = (bf16[128,1024]{1,0:T(8,128)(2,1)S(1)}, bf16[128,1024]{1,0:T(8,128)(2,1)S(1)}, u32[]{:S(2)}, u32[]{:S(2)}) collective-permute-start(bf16[128,1024]{1,0:T(8,128)(2,1)S(1)} %collective-permute-done.10.refs_3_), channel_id=1, source_target_pairs={{8,12},{9,13},{10,14},{11,15},{24,28},{25,29},{26,30},{27,31}} | collective-permute-start | bytes 786440 | tf_op jit(solution)/shard_map/ppermute | solution.py:292
  89.7 11.0 %collective-permute-start.8 = (bf16[128,1024]{1,0:T(8,128)(2,1)S(1)}, bf16[128,1024]{1,0:T(8,128)(2,1)S(1)}, u32[]{:S(2)}, u32[]{:S(2)}) collective-permute-start(bf16[128,1024]{1,0:T(8,128)(2,1)S(1)} %collective-permute-done.4.refs_2_), channel_id=1, source_target_pairs={{0,2},{1,3},{2,0},{3,1},{4,6},{5,7},{6,4},{7,5},{8,10},{9,11},{10,... | collective-permute-start | bytes 786440 | tf_op jit(solution)/shard_map/ppermute | solution.py:292
where the time goes:
time: 126 us; the launch traced here: 123 us
  Pallas kernels  107 us (85%)
  starting transfers between devices  11.6 us (9%)
  local copies, waits for them, and re-layouts  3.29 us (3%)
    pallas_call x7, Pallas kernels, levels(): pl.pallas_call(partial(attend, stride, moves, [[block for _, block in kvs...  107 us
    ppermute x12, starting transfers between devices, send(): return lax.ppermute(x, 'tp', full)  11.6 us
  transfers between devices with their start and end apart: 12, of which 0 were waited for; matrix products, arithmetic and copies ran while one was open for 1% of the time, Pallas kernels for 69%

commit v1 on v0

v1 whole, which is shorter than its diff:
```python
from functools import partial

import jax
import jax.numpy as jnp
from jax import lax
from jax.experimental import pallas as pl
from jax.experimental.pallas import tpu as pltpu
from jax.sharding import PartitionSpec as P

HD = 128
SPAN = 8
TILE = 32
NEG = -1e30
SCALE = HD ** (-0.5)
FACTOR = SCALE * 1.4426950408889634
SMALLEST, LARGEST = 2.0 ** -60, 2.0 ** 100
STATE = HD + 8
VROWS = HD + 16
TOTAL = HD
UNIT = 4
STEP = 2
VMEM = 20 * 1024 * 1024


def parent_of(table_ref, segment):
    return table_ref[1 + segment]


def count_of(table_ref, segment):
    return table_ref[1 + (table_ref.shape[0] - 1) // 2 + segment]


def is_ancestor(table_ref, me, source):
    current = me
    hit = jnp.int32(0)
    for _ in range(SPAN - 1):
        current = jnp.where(current >= 0, parent_of(table_ref, jnp.maximum(current, 0)), -1)
        hit = jnp.where(current == source, 1, hit)
    return jnp.where(source >= 0, hit, 0)


def source_of(me, stride, shift, swap):
    offset = me // stride
    base = offset
    if swap:
        base = jnp.where(offset % 2 == 0, offset + 1, offset - 1)
    base = base - shift
    return jnp.where(base >= 0, base * stride + me % stride, -1)


def live_keys(table_ref, me, stride, move):
    if move is None:
        return count_of(table_ref, me)
    source = source_of(me, stride, *move)
    length = count_of(table_ref, jnp.maximum(source, 0))
    return jnp.where(is_ancestor(table_ref, me, source) > 0, length, 0)


def attend(stride, moves, fold, blocks, parts, first, last, table_ref, *refs):
    refs = list(refs)
    many, n = len(parts), len(fold)
    if first:
        q_ref = refs.pop(0)
    else:
        qt_refs = [refs.pop(0) for _ in parts]
        old_refs = [refs.pop(0) for _ in parts]
    kv_refs = [[refs.pop(0) for _ in moves] for _ in parts]
    if last:
        if parts[0] > 0:
            refs.pop(0)
        out_ref = refs.pop(0)
    else:
        if first:
            qt_refs = [refs.pop(0) for _ in parts]
        new_refs = [refs.pop(0) for _ in parts]
    k_buf, v_buf, bad_buf = refs

    me = table_ref[0]
    count = count_of(table_ref, me)
    held, _, across_all = qt_refs[0].shape
    rows = v_buf.shape[2] // n
    tiles_max = rows // TILE
    lanes = across_all // tiles_max
    group = lanes // TILE
    tiles = (count + TILE - 1) // TILE
    steps = held // STEP
    head = (pl.program_id(0) % steps) * STEP
    turn_of = pl.program_id(0) // steps
    lengths = {l: live_keys(table_ref, me, stride, moves[l]) for l in fold}

    def key_value(i, l, h):
        of = slice(blocks[i][l] * rows, (blocks[i][l] + 1) * rows)
        base = pl.multiple_of((head + h) * 2 * HD, 2 * HD)
        return kv_refs[i][l][of, pl.ds(base, HD)], kv_refs[i][l][of, pl.ds(base + HD, HD)]

    def fill(i):
        j = lax.broadcasted_iota(jnp.int32, (VROWS - HD, rows), 1)
        sub = lax.broadcasted_iota(jnp.int32, (VROWS - HD, rows), 0)
        for at, l in enumerate(fold):
            to = slice(at * rows, (at + 1) * rows)
            inside = jnp.where(j < lengths[l], 1.0, 0.0)
            for h in range(STEP):
                key, value = key_value(i, l, h)
                k_buf[h, to, :] = key
                v_buf[h, :HD, to] = value.T * inside[:1].astype(jnp.bfloat16)
                v_buf[h, HD:, to] = jnp.where(sub == 0, inside, 0.0).astype(jnp.bfloat16)

    def across(t, k=1):
        if isinstance(t, int):
            return slice(t * lanes, (t + k) * lanes)
        return pl.ds(pl.multiple_of(t * lanes, lanes), k * lanes)

    def down(t):
        if isinstance(t, int):
            return slice(t * TILE, (t + 1) * TILE)
        return pl.ds(pl.multiple_of(t * TILE, TILE), TILE)

    def slot(t, shape):
        lane = lax.broadcasted_iota(jnp.int32, shape, 1)
        return lane % TILE + (lane // lanes + t) * TILE

    def turned(i, h, t, k):
        if first:
            base = (parts[i] * held + head + h) * group * HD
            for u in range(k):
                heads = [
                    q_ref[down(t + u), pl.ds(pl.multiple_of(base + g * HD, HD), HD)] for g in range(group)
                ]
                qt_refs[i][head + h, :, across(t + u)] = jnp.concatenate(heads, axis=0).T
        return qt_refs[i][head + h, :, across(t, k)]

    def scores(i, h, t, k):
        return jnp.dot(k_buf[h], turned(i, h, t, k), preferred_element_type=jnp.float32)

    def write(h, t, k, mixed, total):
        live = slot(t, (1, k * lanes)) < count
        result = (mixed * jnp.where(live, 1.0 / total, 0.0)).astype(out_ref.dtype).T
        for u in range(k):
            for g in range(group):
                at = u * lanes + g * TILE
                to = (h * group + g) * HD
                out_ref[down(t + u), to:to + HD] = result[at:at + TILE]

    def unshifted(i, h, t, k, s):
        w = jnp.exp2(s * FACTOR)
        if first:
            j = lax.broadcasted_iota(jnp.int32, (rows, k * lanes), 0)
            w = jnp.where(j <= slot(t, (rows, k * lanes)), w, 0.0)
        mixed = jnp.dot(v_buf[h], w.astype(jnp.bfloat16), preferred_element_type=jnp.float32)[:STATE]
        if not first:
            mixed = mixed + old_refs[i][head + h, :, across(t, k)]
        if last:
            total = mixed[TOTAL:TOTAL + 1]
            good = (total >= SMALLEST) & (total <= LARGEST)
            bad_buf[h:h + 1, across(t, k)] = jnp.where(good, 0.0, 1.0)
            write(h, t, k, mixed[:HD], total)
        else:
            new_refs[i][head + h, :, across(t, k)] = mixed

    def settle(i, k):
        for h in range(STEP):
            mixed = old_refs[i][head + h, :, across(0, k)]
            total = mixed[TOTAL:TOTAL + 1]
            good = (total >= SMALLEST) & (total <= LARGEST)
            bad_buf[h:h + 1, across(0, k)] = jnp.where(good, 0.0, 1.0)
            write(h, 0, k, mixed[:HD], total)

    def run(i, k):
        units = [(i, h, t, min(UNIT, k - t)) for h in range(STEP) for t in range(0, k, UNIT)]
        s = scores(*units[0])
        for at, unit in enumerate(units):
            following = scores(*units[at + 1]) if at + 1 < len(units) else None
            unshifted(*unit, s)
            s = following

    def shifted(i, h, t, _):
        q = qt_refs[i][head + h, :, across(t)]
        j = lax.broadcasted_iota(jnp.int32, (rows, lanes), 0)
        pieces = []
        for l, move in enumerate(moves):
            s = jnp.dot(key_value(i, l, h)[0], q, preferred_element_type=jnp.float32)
            allowed = j < live_keys(table_ref, me, stride, move)
            if move is None:
                allowed = allowed & (j <= slot(t, (rows, lanes)))
            pieces.append(jnp.where(allowed, s, NEG))
        top = jnp.max(pieces[0], axis=0, keepdims=True)
        for s in pieces[1:]:
            top = jnp.maximum(top, jnp.max(s, axis=0, keepdims=True))
        mixed = jnp.zeros((HD, lanes), jnp.float32)
        total = jnp.zeros((1, lanes), jnp.float32)
        for l, s in enumerate(pieces):
            w = jnp.exp2((s - top) * FACTOR)
            total = total + jnp.sum(w, axis=0, keepdims=True)
            value_t = key_value(i, l, h)[1].T
            mixed = mixed + jnp.dot(value_t, w.astype(jnp.bfloat16), preferred_element_type=jnp.float32)
        write(h, t, 1, mixed, total)
        return 0

    def safely(i):
        for h in range(STEP):
            lax.fori_loop(0, tiles, partial(shifted, i, h), 0)

    def keep(i):
        for h in range(STEP):
            new_refs[i][head + h] = old_refs[i][head + h]

    some = sum(lengths.values()) > 0
    for i in range(many):
        here = turn_of == i if many > 1 else count > 0
        mine = here & some
        pl.when(mine)(partial(fill, i))
        if last:
            bad_buf[...] = jnp.zeros(bad_buf.shape, jnp.float32)
        for k in range(1, tiles_max + 1):
            pl.when(mine & (tiles == k))(partial(run, i, k))
            if last:
                pl.when(here & jnp.logical_not(some) & (tiles == k))(partial(settle, i, k))
        if last:
            pl.when(here & (jnp.max(bad_buf[:STEP, :]) > 0.0))(partial(safely, i))
        elif not first:
            pl.when(here & jnp.logical_not(some))(partial(keep, i))

    if last:
        def clear(t, _):
            out_ref[down(t), :] = jnp.zeros((TILE, out_ref.shape[1]), out_ref.dtype)
            return 0

        lax.fori_loop(tiles, tiles_max, clear, 0)


def levels(stride, table, queries, kv_heads, moves, kvs, state, parts=(0, 1), fold=None, last=False, into=None, begin=False):
    rows, width = queries.shape
    group = width // HD // kv_heads
    half = kv_heads // 2
    tiles_max = rows // TILE
    lanes = group * TILE
    first = state is None or begin
    steps = half // STEP
    fold = list(range(len(moves))) if fold is None else fold
    n, many = len(fold), len(parts)
    whole = pl.BlockSpec(memory_space=pltpu.VMEM)
    if first:
        operands = [queries]
    else:
        operands = [state[part][0] for part in parts] + [state[part][1] for part in parts]
    operands += [array for part in parts for array, _ in kvs[part]]
    specs = [whole] * len(operands)
    aliases = {}
    if into is not None:
        specs.append(pl.BlockSpec(memory_space=pl.ANY))
        aliases = {1 + len(operands): 0}
        operands.append(into)
    if last:
        out_specs = pl.BlockSpec((rows, STEP * group * HD), lambda k, *_: (0, k + parts[0] * steps))
        out_shape = jax.ShapeDtypeStruct((rows, width), jnp.bfloat16)
    else:
        turned = jax.ShapeDtypeStruct((half, HD, tiles_max * lanes), jnp.bfloat16)
        held = jax.ShapeDtypeStruct((half, STATE, tiles_max * lanes), jnp.float32)
        out_shape = [turned] * (many if first else 0) + [held] * many
        out_specs = [whole] * len(out_shape)
    result = pl.pallas_call(
        partial(attend, stride, moves, fold, [[block for _, block in kvs[part]] for part in parts], parts, first, last),
        grid_spec=pltpu.PrefetchScalarGridSpec(
            num_scalar_prefetch=1,
            grid=(many * steps,),
            in_specs=specs,
            out_specs=out_specs,
            scratch_shapes=[
                pltpu.VMEM((STEP, n * rows, HD), jnp.bfloat16),
                pltpu.VMEM((STEP, VROWS, n * rows), jnp.bfloat16),
                pltpu.VMEM((8, tiles_max * lanes), jnp.float32),
            ],
        ),
        out_shape=out_shape,
        input_output_aliases=aliases,
        compiler_params=pltpu.CompilerParams(vmem_limit_bytes=VMEM),
        cost_estimate=pl.CostEstimate(
            flops=2 * rows * rows * width * n * many,
            bytes_accessed=rows * width * many,
            transcendentals=rows * rows * width // HD * n // 2 * many,
        ),
        name="levels_" + str(n) + ("_first" if first else "_last" if last else ""),
    )(table, *operands)
    if last:
        return result
    state = dict(state or {})
    for at, part in enumerate(parts):
        state[part] = (result[at], result[many + at]) if first else (state[part][0], result[at])
    return state


def per_device(queries, keyvals, parent, counts):
    rows, width = queries.shape
    kv_heads = keyvals.shape[1] // (2 * HD)
    half = kv_heads // 2
    segments = lax.axis_size("tp")
    stride = segments // SPAN
    me = lax.axis_index("tp").reshape(1).astype(jnp.int32)
    table = jnp.concatenate([me, parent, counts])

    def send(x, pairs):
        full = [(a * stride + t, b * stride + t) for a, b in pairs for t in range(stride)]
        return lax.ppermute(x, "tp", full)

    def kernel(moves, kvs, state, **more):
        return levels(stride, table, queries, kv_heads, moves, kvs, state, **more)

    def halves(*arrays):
        return [[(array, part) for array in arrays] for part in (0, 1)]

    swap = [(o, o ^ 1) for o in range(SPAN)]
    up = [(o, (o + 2) % SPAN) for o in range(SPAN)]
    swap3 = [(o, o ^ 1) for o in range(4, SPAN)]
    swap4 = [(o, o ^ 1) for o in range(6, SPAN)]
    up3 = [(o, o + 2) for o in range(4, SPAN - 2)]
    cut = half * 2 * HD
    hold = lax.optimization_barrier
    m1 = [(2, False), (0, True)]
    m2 = [(4, False), (2, True)]
    m3 = [(6, False), (4, True)]
    m4 = [(6, True)]
    every = [None] + m1 + m2 + m3 + m4
    a, b = keyvals[:, :cut], keyvals[:, cut:]
    ax1, az1 = send(a, swap), send(a, up)
    bx1, bz1 = send(b, swap), send(b, up)
    state = kernel([None], [[(a, 0)], None], None, parts=(0,))
    az1, ax1, state = hold((az1, ax1, state))
    ax2 = send(az1, swap)
    az2 = send(az1, up)
    state = kernel([None], [None, [(b, 0)]], state, parts=(1,), begin=True)
    bz1, bx1, state = hold((bz1, bx1, state))
    bx2 = send(bz1, swap)
    bz2 = send(bz1, up)
    state = kernel(m1, [[(az1, 0), (ax1, 0)], [(bz1, 0), (bx1, 0)]], state)
    az2, ax2, state = hold((az2, ax2, state))
    ax3 = send(az2, swap)
    az3 = send(az2, up3)
    state = kernel(m2, [[(az2, 0), (ax2, 0)], None], state, parts=(0,))
    bz2, bx2, state = hold((bz2, bx2, state))
    bx3 = send(bz2, swap)
    bz3 = send(bz2, up3)
    state = kernel(m2, [None, [(bz2, 0), (bx2, 0)]], state, parts=(1,))
    az3, ax3, state = hold((az3, ax3, state))
    a4 = send(az3, swap)
    state = kernel(m3, [[(az3, 0), (ax3, 0)], None], state, parts=(0,))
    bz3, bx3, state = hold((bz3, bx3, state))
    b4 = send(bx3, up3)
    state = kernel(m3, [None, [(bz3, 0), (bx3, 0)]], state, parts=(1,))
    of_a = [(a, 0), (az1, 0), (ax1, 0), (az2, 0), (ax2, 0), (az3, 0), (ax3, 0), (a4, 0)]
    of_b = [(b, 0), (bz1, 0), (bx1, 0), (bz2, 0), (bx2, 0), (bz3, 0), (bx3, 0), (b4, 0)]
    out = kernel(every, [of_a, None], state, parts=(0,), fold=[7], last=True)
    return kernel(every, [None, of_b], state, parts=(1,), fold=[7], last=True, into=out)

def solution(mesh):
    in_specs = (P(("rep", "tp"), None), P(("rep", "tp"), None), P("rep"), P("rep"))
    out_specs = P(("rep", "tp"), None)
    return jax.shard_map(
        per_device, mesh=mesh, in_specs=in_specs, out_specs=out_specs, check_vma=False
    )
```

time: 126 us -> 91.8 us (0.73)
  the two profiles are of different devices: /device:TPU:24 before, /device:TPU:29 now
where the time goes in v1:
time: 91.8 us; the launch traced here: 90.6 us
  Pallas kernels  71.4 us (78%)
  starting transfers between devices  12.4 us (14%)
  local copies, waits for them, and re-layouts  3.25 us (4%)
  waiting for transfers between devices  2.64 us (3%)
    pallas_call x9, Pallas kernels, levels(): pl.pallas_call(partial(attend, stride, moves, fold, [[block for _, block...  71.4 us
    ppermute x14, starting transfers between devices, send(): return lax.ppermute(x, 'tp', full)  12.4 us
    ppermute x14, waiting for transfers between devices, send(): return lax.ppermute(x, 'tp', full)  2.64 us
    unnamed x2, local copies, waits for them, and re-layouts  2.19 us
  transfers between devices with their start and end apart: 14, of which 2 were waited for; matrix products, arithmetic and copies ran while one was open for 1% of the time, Pallas kernels for 52%

profile of v1, /device:TPU:29, one launch (start us, length us, event | category | flops | bytes accessed | tf_op | source)
XLA Modules:
  0.0 90.6 jit_solution(7871149203082218333)
XLA Ops:
  0.0 1.1 %fusion = (bf16[128,1024]{1,0:T(8,128)(2,1)S(1)}, bf16[128,1024]{1,0:T(8,128)(2,1)S(1)}) fusion(bf16[128,2048]{1,0:T(8,128)(2,1)} %param.5), kind=kLoop, calls=%fused_computation.1 | loop fusion | bytes 1048576 | tf_op jit(solution)/shard_map/slice | solution.py:323
  1.1 1.3 %collective-permute-start.3 = (bf16[128,1024]{1,0:T(8,128)(2,1)S(1)}, bf16[128,1024]{1,0:T(8,128)(2,1)S(1)}, u32[]{:S(2)}, u32[]{:S(2)}) collective-permute-start(bf16[128,1024]{1,0:T(8,128)(2,1)S(1)} %get-tuple-element.85.refs_1_.refs_2_), channel_id=1, source_target_pairs={{0,2},{1,3},{2,0},{3,1},{4,6},{5,7},{6,4},{7,5},{8,10},{9,11},{10,... | collective-permute-start | bytes 786440 | tf_op jit(solution)/shard_map/ppermute | solution.py:303
  2.4 1.2 %collective-permute-start = (bf16[128,1024]{1,0:T(8,128)(2,1)S(1)}, bf16[128,1024]{1,0:T(8,128)(2,1)S(1)}, u32[]{:S(2)}, u32[]{:S(2)}) collective-permute-start(bf16[128,1024]{1,0:T(8,128)(2,1)S(1)} %get-tuple-element.86.refs_1_.refs_2_), channel_id=1, source_target_pairs={{0,4},{1,5},{2,6},{3,7},{4,8},{5,9},{6,10},{7,11},{8,12},{9,13},{1... | collective-permute-start | bytes 786440 | tf_op jit(solution)/shard_map/ppermute | solution.py:303
  3.8 0.7 pad_add_fusion.table_ref
  4.6 2.2 %copy-done = bf16[128,16384]{1,0:T(8,128)(2,1)S(1)} copy-done((bf16[128,16384]{1,0:T(8,128)(2,1)S(1)}, bf16[128,16384]{1,0:T(8,128)(2,1)}, u32[]{:S(2)}) %copy-start) | copy-done | bytes 4194328
  6.8 2.6 %levels_1_first.2 = (bf16[4,128,2048]{2,1,0:T(8,128)(2,1)S(1)}, f32[4,136,2048]{2,1,0:T(8,128)S(1)}) custom-call(s32[33]{0:T(128)S(1)} %pad_add_fusion.table_ref, bf16[128,16384]{1,0:T(8,128)(2,1)S(1)} %copy-done, bf16[128,1024]{1,0:T(8,128)(2,1)S(1)} %get-tuple-element.85.refs_1_.refs_2_), custom_call_target="tpu_custom_call" | custom-call | flops 536870912 | bytes 2097152 | tf_op jit(solution)/shard_map/levels_1_first/pallas_call | solution.py:261
  9.4 1.0 %collective-permute-start.6 = (bf16[128,1024]{1,0:T(8,128)(2,1)S(1)}, bf16[128,1024]{1,0:T(8,128)(2,1)S(1)}, u32[]{:S(2)}, u32[]{:S(2)}) collective-permute-start(bf16[128,1024]{1,0:T(8,128)(2,1)S(1)} %collective-permute-done.2.refs_4_.refs_3_), channel_id=1, source_target_pairs={{0,4},{1,5},{2,6},{3,7},{4,8},{5,9},{6,10},{7,11},{8,12},{9,13},{1... | collective-permute-start | bytes 786440 | tf_op jit(solution)/shard_map/ppermute | solution.py:303
  10.4 1.6 %collective-permute-start.7 = (bf16[128,1024]{1,0:T(8,128)(2,1)S(1)}, bf16[128,1024]{1,0:T(8,128)(2,1)S(1)}, u32[]{:S(2)}, u32[]{:S(2)}) collective-permute-start(bf16[128,1024]{1,0:T(8,128)(2,1)S(1)} %collective-permute-done.2.refs_4_.refs_3_), channel_id=1, source_target_pairs={{0,2},{1,3},{2,0},{3,1},{4,6},{5,7},{6,4},{7,5},{8,10},{9,11},{10,... | collective-permute-start | bytes 786440 | tf_op jit(solution)/shard_map/ppermute | solution.py:303
  12.0 2.6 %levels_1_first.3 = (bf16[4,128,2048]{2,1,0:T(8,128)(2,1)S(1)}, f32[4,136,2048]{2,1,0:T(8,128)S(1)}) custom-call(s32[33]{0:T(128)S(1)} %pad_add_fusion.table_ref, bf16[128,16384]{1,0:T(8,128)(2,1)S(1)} %copy-done, bf16[128,1024]{1,0:T(8,128)(2,1)S(1)} %get-tuple-element.86.refs_1_.refs_2_), custom_call_target="tpu_custom_call" | custom-call | flops 536870912 | bytes 2097152 | tf_op jit(solution)/shard_map/levels_1_first/pallas_call | solution.py:261
  14.7 1.1 %collective-permute-start.4 = (bf16[128,1024]{1,0:T(8,128)(2,1)S(1)}, bf16[128,1024]{1,0:T(8,128)(2,1)S(1)}, u32[]{:S(2)}, u32[]{:S(2)}) collective-permute-start(bf16[128,1024]{1,0:T(8,128)(2,1)S(1)} %collective-permute-done.refs_6_.refs_3_), channel_id=1, source_target_pairs={{0,4},{1,5},{2,6},{3,7},{4,8},{5,9},{6,10},{7,11},{8,12},{9,13},{1... | collective-permute-start | bytes 786440 | tf_op jit(solution)/shard_map/ppermute | solution.py:303
  15.8 1.2 %collective-permute-start.5 = (bf16[128,1024]{1,0:T(8,128)(2,1)S(1)}, bf16[128,1024]{1,0:T(8,128)(2,1)S(1)}, u32[]{:S(2)}, u32[]{:S(2)}) collective-permute-start(bf16[128,1024]{1,0:T(8,128)(2,1)S(1)} %collective-permute-done.refs_6_.refs_3_), channel_id=1, source_target_pairs={{0,2},{1,3},{2,0},{3,1},{4,6},{5,7},{6,4},{7,5},{8,10},{9,11},{10,... | collective-permute-start | bytes 786440 | tf_op jit(solution)/shard_map/ppermute | solution.py:303
  17.0 5.8 %levels_2.5 = (f32[4,136,2048]{2,1,0:T(8,128)S(1)}, f32[4,136,2048]{2,1,0:T(8,128)S(1)}) custom-call(s32[33]{0:T(128)S(1)} %pad_add_fusion.table_ref, bf16[4,128,2048]{2,1,0:T(8,128)(2,1)S(1)} %get-tuple-element.83.refs_0_, bf16[4,128,2048]{2,1,0:T(8,128)(2,1)S(1)} %get-tuple-element.79.refs_1_.refs_0_, f32[4,136,2048]{2,1,0:T(8,128)S(1)} %get-tuple-element.55.refs_2_, ...), custom_call_target="tpu_custom_call" | custom-call | flops 2147483648 | bytes 4194304 | tf_op jit(solution)/shard_map/levels_2/pallas_call | solution.py:261
  22.9 1.5 %collective-permute-start.10 = (bf16[128,1024]{1,0:T(8,128)(2,1)S(1)}, bf16[128,1024]{1,0:T(8,128)(2,1)S(1)}, u32[]{:S(2)}, u32[]{:S(2)}) collective-permute-start(bf16[128,1024]{1,0:T(8,128)(2,1)S(1)} %collective-permute-done.6.refs_2_.refs_5_), channel_id=1, source_target_pairs={{8,12},{9,13},{10,14},{11,15},{24,28},{25,29},{26,30},{27,31}} | collective-permute-start | bytes 786440 | tf_op jit(solution)/shard_map/ppermute | solution.py:303
  24.4 3.1 %levels_2.6.refs_1_ = f32[4,136,2048]{2,1,0:T(8,128)S(1)} custom-call(s32[33]{0:T(128)S(1)} %pad_add_fusion.table_ref, bf16[4,128,2048]{2,1,0:T(8,128)(2,1)S(1)} %get-tuple-element.83.refs_0_, f32[4,136,2048]{2,1,0:T(8,128)S(1)} %get-tuple-element.62.refs_1_, bf16[128,1024]{1,0:T(8,128)(2,1)S(1)} %collective-permute-done.6.refs_2_.refs_5_, ...), custom_call_target="tpu_custom_call" | custom-call | flops 1073741824 | bytes 2097152 | tf_op jit(solution)/shard_map/levels_2/pallas_call | solution.py:261
  27.6 1.3 %collective-permute-start.8 = (bf16[128,1024]{1,0:T(8,128)(2,1)S(1)}, bf16[128,1024]{1,0:T(8,128)(2,1)S(1)}, u32[]{:S(2)}, u32[]{:S(2)}) collective-permute-start(bf16[128,1024]{1,0:T(8,128)(2,1)S(1)} %collective-permute-done.4.refs_2_.refs_5_), channel_id=1, source_target_pairs={{8,12},{9,13},{10,14},{11,15},{24,28},{25,29},{26,30},{27,31}} | collective-permute-start | bytes 786440 | tf_op jit(solution)/shard_map/ppermute | solution.py:303
  28.9 0.3 collective-permute-start.9
  29.2 3.1 %levels_2.7.refs_1_ = f32[4,136,2048]{2,1,0:T(8,128)S(1)} custom-call(s32[33]{0:T(128)S(1)} %pad_add_fusion.table_ref, bf16[4,128,2048]{2,1,0:T(8,128)(2,1)S(1)} %get-tuple-element.79.refs_1_.refs_0_, f32[4,136,2048]{2,1,0:T(8,128)S(1)} %get-tuple-element.71.refs_1_, bf16[128,1024]{1,0:T(8,128)(2,1)S(1)} %collective-permute-done.4.refs_2_.refs_5_, ...), custom_call_target="tpu_custom_call" | custom-call | flops 1073741824 | bytes 2097152 | tf_op jit(solution)/shard_map/levels_2/pallas_call | solution.py:261
  32.5 3.1 %levels_2.8.refs_1_ = f32[4,136,2048]{2,1,0:T(8,128)S(1)} custom-call(s32[33]{0:T(128)S(1)} %pad_add_fusion.table_ref, bf16[4,128,2048]{2,1,0:T(8,128)(2,1)S(1)} %get-tuple-element.83.refs_0_, f32[4,136,2048]{2,1,0:T(8,128)S(1)} %levels_2.6.refs_1_, bf16[128,1024]{1,0:T(8,128)(2,1)S(1)} %collective-permute-done.10.refs_2_.refs_7_, ...), custom_call_target="tpu_custom_call" | custom-call | flops 1073741824 | bytes 2097152 | tf_op jit(solution)/shard_map/levels_2/pallas_call | solution.py:261
  35.6 1.8 %collective-permute-done.8.refs_2_.refs_7_ = bf16[128,1024]{1,0:T(8,128)(2,1)S(1)} collective-permute-done((bf16[128,1024]{1,0:T(8,128)(2,1)S(1)}, bf16[128,1024]{1,0:T(8,128)(2,1)S(1)}, u32[]{:S(2)}, u32[]{:S(2)}) %collective-permute-start.8) | collective-permute-done | bytes 262176 | tf_op jit(solution)/shard_map/ppermute | solution.py:303
  37.4 1.5 %collective-permute-start.12 = (bf16[128,1024]{1,0:T(8,128)(2,1)S(1)}, bf16[128,1024]{1,0:T(8,128)(2,1)S(1)}, u32[]{:S(2)}, u32[]{:S(2)}) collective-permute-start(bf16[128,1024]{1,0:T(8,128)(2,1)S(1)} %collective-permute-done.9.refs_3_.refs_8_), channel_id=1, source_target_pairs={{8,12},{9,13},{10,14},{11,15},{24,28},{25,29},{26,30},{27,31}} | collective-permute-start | bytes 786440 | tf_op jit(solution)/shard_map/ppermute | solution.py:303
  38.9 3.1 %levels_2.9.refs_1_ = f32[4,136,2048]{2,1,0:T(8,128)S(1)} custom-call(s32[33]{0:T(128)S(1)} %pad_add_fusion.table_ref, bf16[4,128,2048]{2,1,0:T(8,128)(2,1)S(1)} %get-tuple-element.79.refs_1_.refs_0_, f32[4,136,2048]{2,1,0:T(8,128)S(1)} %levels_2.7.refs_1_, bf16[128,1024]{1,0:T(8,128)(2,1)S(1)} %collective-permute-done.8.refs_2_.refs_7_, ...), custom_call_target="tpu_custom_call" | custom-call | flops 1073741824 | bytes 2097152 | tf_op jit(solution)/shard_map/levels_2/pallas_call | solution.py:261
  42.1 0.8 collective-permute-done.13.refs_9_
  42.9 23.7 %levels_1_last.2.refs_10_ = bf16[128,16384]{1,0:T(8,128)(2,1)} custom-call(s32[33]{0:T(128)S(1)} %pad_add_fusion.table_ref, bf16[4,128,2048]{2,1,0:T(8,128)(2,1)S(1)} %get-tuple-element.83.refs_0_, f32[4,136,2048]{2,1,0:T(8,128)S(1)} %levels_2.8.refs_1_, bf16[128,1024]{1,0:T(8,128)(2,1)S(1)} %get-tuple-element.85.refs_1_.refs_2_, ...), custom_call_target="tpu_custom_call" | custom-call | flops 536870912 | bytes 2097152 | tf_op jit(solution)/shard_map/levels_1_last/pallas_call | solution.py:261
  66.6 24.0 %levels_1_last.3 = bf16[128,16384]{1,0:T(8,128)(2,1)} custom-call(s32[33]{0:T(128)S(1)} %pad_add_fusion.table_ref, bf16[4,128,2048]{2,1,0:T(8,128)(2,1)S(1)} %get-tuple-element.79.refs_1_.refs_0_, f32[4,136,2048]{2,1,0:T(8,128)S(1)} %levels_2.9.refs_1_, bf16[128,1024]{1,0:T(8,128)(2,1)S(1)} %get-tuple-element.86.refs_1_.refs_2_, ...), custom_call_target="tpu_custom_call", output_to_operand_aliasing={{}: (11, {})} | custom-call | flops 536870912 | bytes 2097152 | tf_op jit(solution)/shard_map/levels_1_last/pallas_call | solution.py:261
  (17 shorter events, 0.5 us)
Async XLA Ops:
  1.1 8.4 %collective-permute-start.2 = (bf16[128,1024]{1,0:T(8,128)(2,1)S(1)}, bf16[128,1024]{1,0:T(8,128)(2,1)S(1)}, u32[]{:S(2)}, u32[]{:S(2)}) collective-permute-start(bf16[128,1024]{1,0:T(8,128)(2,1)S(1)} %get-tuple-element.85.refs_1_.refs_2_), channel_id=1, source_target_pairs={{0,4},{1,5},{2,6},{3,7},{4,8},{5,9},{6,10},{7,11},{8,12},{9,13},{1... | collective-permute-start | bytes 786440 | tf_op jit(solution)/shard_map/ppermute | solution.py:303
  1.1 8.3 %collective-permute-start.3 = (bf16[128,1024]{1,0:T(8,128)(2,1)S(1)}, bf16[128,1024]{1,0:T(8,128)(2,1)S(1)}, u32[]{:S(2)}, u32[]{:S(2)}) collective-permute-start(bf16[128,1024]{1,0:T(8,128)(2,1)S(1)} %get-tuple-element.85.refs_1_.refs_2_), channel_id=1, source_target_pairs={{0,2},{1,3},{2,0},{3,1},{4,6},{5,7},{6,4},{7,5},{8,10},{9,11},{10,... | collective-permute-start | bytes 786440 | tf_op jit(solution)/shard_map/ppermute | solution.py:303
  2.4 12.2 %collective-permute-start = (bf16[128,1024]{1,0:T(8,128)(2,1)S(1)}, bf16[128,1024]{1,0:T(8,128)(2,1)S(1)}, u32[]{:S(2)}, u32[]{:S(2)}) collective-permute-start(bf16[128,1024]{1,0:T(8,128)(2,1)S(1)} %get-tuple-element.86.refs_1_.refs_2_), channel_id=1, source_target_pairs={{0,4},{1,5},{2,6},{3,7},{4,8},{5,9},{6,10},{7,11},{8,12},{9,13},{1... | collective-permute-start | bytes 786440 | tf_op jit(solution)/shard_map/ppermute | solution.py:303
  3.6 11.1 %collective-permute-start.1 = (bf16[128,1024]{1,0:T(8,128)(2,1)S(1)}, bf16[128,1024]{1,0:T(8,128)(2,1)S(1)}, u32[]{:S(2)}, u32[]{:S(2)}) collective-permute-start(bf16[128,1024]{1,0:T(8,128)(2,1)S(1)} %get-tuple-element.86.refs_1_.refs_2_), channel_id=1, source_target_pairs={{0,2},{1,3},{2,0},{3,1},{4,6},{5,7},{6,4},{7,5},{8,10},{9,11},{10,... | collective-permute-start | bytes 786440 | tf_op jit(solution)/shard_map/ppermute | solution.py:303
  4.6 2.2 %copy-start = (bf16[128,16384]{1,0:T(8,128)(2,1)S(1)}, bf16[128,16384]{1,0:T(8,128)(2,1)}, u32[]{:S(2)}) copy-start(bf16[128,16384]{1,0:T(8,128)(2,1)} %refs_0_.3) | copy-start | bytes 12582916
  9.4 13.4 %collective-permute-start.6 = (bf16[128,1024]{1,0:T(8,128)(2,1)S(1)}, bf16[128,1024]{1,0:T(8,128)(2,1)S(1)}, u32[]{:S(2)}, u32[]{:S(2)}) collective-permute-start(bf16[128,1024]{1,0:T(8,128)(2,1)S(1)} %collective-permute-done.2.refs_4_.refs_3_), channel_id=1, source_target_pairs={{0,4},{1,5},{2,6},{3,7},{4,8},{5,9},{6,10},{7,11},{8,12},{9,13},{1... | collective-permute-start | bytes 786440 | tf_op jit(solution)/shard_map/ppermute | solution.py:303
  10.4 12.4 %collective-permute-start.7 = (bf16[128,1024]{1,0:T(8,128)(2,1)S(1)}, bf16[128,1024]{1,0:T(8,128)(2,1)S(1)}, u32[]{:S(2)}, u32[]{:S(2)}) collective-permute-start(bf16[128,1024]{1,0:T(8,128)(2,1)S(1)} %collective-permute-done.2.refs_4_.refs_3_), channel_id=1, source_target_pairs={{0,2},{1,3},{2,0},{3,1},{4,6},{5,7},{6,4},{7,5},{8,10},{9,11},{10,... | collective-permute-start | bytes 786440 | tf_op jit(solution)/shard_map/ppermute | solution.py:303
  14.7 12.9 %collective-permute-start.4 = (bf16[128,1024]{1,0:T(8,128)(2,1)S(1)}, bf16[128,1024]{1,0:T(8,128)(2,1)S(1)}, u32[]{:S(2)}, u32[]{:S(2)}) collective-permute-start(bf16[128,1024]{1,0:T(8,128)(2,1)S(1)} %collective-permute-done.refs_6_.refs_3_), channel_id=1, source_target_pairs={{0,4},{1,5},{2,6},{3,7},{4,8},{5,9},{6,10},{7,11},{8,12},{9,13},{1... | collective-permute-start | bytes 786440 | tf_op jit(solution)/shard_map/ppermute | solution.py:303
  15.8 11.8 %collective-permute-start.5 = (bf16[128,1024]{1,0:T(8,128)(2,1)S(1)}, bf16[128,1024]{1,0:T(8,128)(2,1)S(1)}, u32[]{:S(2)}, u32[]{:S(2)}) collective-permute-start(bf16[128,1024]{1,0:T(8,128)(2,1)S(1)} %collective-permute-done.refs_6_.refs_3_), channel_id=1, source_target_pairs={{0,2},{1,3},{2,0},{3,1},{4,6},{5,7},{6,4},{7,5},{8,10},{9,11},{10,... | collective-permute-start | bytes 786440 | tf_op jit(solution)/shard_map/ppermute | solution.py:303
  22.9 9.5 %collective-permute-start.10 = (bf16[128,1024]{1,0:T(8,128)(2,1)S(1)}, bf16[128,1024]{1,0:T(8,128)(2,1)S(1)}, u32[]{:S(2)}, u32[]{:S(2)}) collective-permute-start(bf16[128,1024]{1,0:T(8,128)(2,1)S(1)} %collective-permute-done.6.refs_2_.refs_5_), channel_id=1, source_target_pairs={{8,12},{9,13},{10,14},{11,15},{24,28},{25,29},{26,30},{27,31}} | collective-permute-start | bytes 786440 | tf_op jit(solution)/shard_map/ppermute | solution.py:303
  24.3 8.0 %collective-permute-start.11 = (bf16[128,1024]{1,0:T(8,128)(2,1)S(1)}, bf16[128,1024]{1,0:T(8,128)(2,1)S(1)}, u32[]{:S(2)}, u32[]{:S(2)}) collective-permute-start(bf16[128,1024]{1,0:T(8,128)(2,1)S(1)} %collective-permute-done.6.refs_2_.refs_5_), channel_id=1, source_target_pairs={{0,2},{1,3},{2,0},{3,1},{4,6},{5,7},{6,4},{7,5},{8,10},{9,11},{10,... | collective-permute-start | bytes 786440 | tf_op jit(solution)/shard_map/ppermute | solution.py:303
  27.6 9.8 %collective-permute-start.8 = (bf16[128,1024]{1,0:T(8,128)(2,1)S(1)}, bf16[128,1024]{1,0:T(8,128)(2,1)S(1)}, u32[]{:S(2)}, u32[]{:S(2)}) collective-permute-start(bf16[128,1024]{1,0:T(8,128)(2,1)S(1)} %collective-permute-done.4.refs_2_.refs_5_), channel_id=1, source_target_pairs={{8,12},{9,13},{10,14},{11,15},{24,28},{25,29},{26,30},{27,31}} | collective-permute-start | bytes 786440 | tf_op jit(solution)/shard_map/ppermute | solution.py:303
  28.9 8.5 %collective-permute-start.9 = (bf16[128,1024]{1,0:T(8,128)(2,1)S(1)}, bf16[128,1024]{1,0:T(8,128)(2,1)S(1)}, u32[]{:S(2)}, u32[]{:S(2)}) collective-permute-start(bf16[128,1024]{1,0:T(8,128)(2,1)S(1)} %collective-permute-done.4.refs_2_.refs_5_), channel_id=1, source_target_pairs={{0,2},{1,3},{2,0},{3,1},{4,6},{5,7},{6,4},{7,5},{8,10},{9,11},{10,... | collective-permute-start | bytes 786440 | tf_op jit(solution)/shard_map/ppermute | solution.py:303
  32.4 10.5 %collective-permute-start.13 = (bf16[128,1024]{1,0:T(8,128)(2,1)S(1)}, bf16[128,1024]{1,0:T(8,128)(2,1)S(1)}, u32[]{:S(2)}, u32[]{:S(2)}) collective-permute-start(bf16[128,1024]{1,0:T(8,128)(2,1)S(1)} %collective-permute-done.10.refs_2_.refs_7_), channel_id=1, source_target_pairs={{0,2},{1,3},{2,0},{3,1},{4,6},{5,7},{6,4},{7,5},{8,10},{9,11},{10,... | collective-permute-start | bytes 786440 | tf_op jit(solution)/shard_map/ppermute | solution.py:303
  37.4 29.2 %collective-permute-start.12 = (bf16[128,1024]{1,0:T(8,128)(2,1)S(1)}, bf16[128,1024]{1,0:T(8,128)(2,1)S(1)}, u32[]{:S(2)}, u32[]{:S(2)}) collective-permute-start(bf16[128,1024]{1,0:T(8,128)(2,1)S(1)} %collective-permute-done.9.refs_3_.refs_8_), channel_id=1, source_target_pairs={{8,12},{9,13},{10,14},{11,15},{24,28},{25,29},{26,30},{27,31}} | collective-permute-start | bytes 786440 | tf_op jit(solution)/shard_map/ppermute | solution.py:303

commit v2 on v1

--- a/solution.py
+++ b/solution.py
@@ -145,7 +145,8 @@
         w = jnp.exp2(s * FACTOR)
         if first:
             j = lax.broadcasted_iota(jnp.int32, (rows, k * lanes), 0)
-            w = jnp.where(j <= slot(t, (rows, k * lanes)), w, 0.0)
+            own = jnp.where(j <= slot(t, (rows, k * lanes)), w[:rows], 0.0)
+            w = jnp.concatenate([own, w[rows:]], axis=0) if n > 1 else own
         mixed = jnp.dot(v_buf[h], w.astype(jnp.bfloat16), preferred_element_type=jnp.float32)[:STATE]
         if not first:
             mixed = mixed + old_refs[i][head + h, :, across(t, k)]
@@ -331,7 +332,7 @@
     bz1, bx1, state = hold((bz1, bx1, state))
     bx2 = send(bz1, swap)
     bz2 = send(bz1, up)
-    state = kernel(m1, [[(az1, 0), (ax1, 0)], [(bz1, 0), (bx1, 0)]], state)
+    state = kernel(m1, [[(az1, 0), (ax1, 0)], [(bz1, 0), (bx1, 0)]], state, parts=(0,))
     az2, ax2, state = hold((az2, ax2, state))
     ax3 = send(az2, swap)
     az3 = send(az2, up3)
@@ -339,7 +340,7 @@
     bz2, bx2, state = hold((bz2, bx2, state))
     bx3 = send(bz2, swap)
     bz3 = send(bz2, up3)
-    state = kernel(m2, [None, [(bz2, 0), (bx2, 0)]], state, parts=(1,))
+    state = kernel(m1 + m2, [None, [(bz1, 0), (bx1, 0), (bz2, 0), (bx2, 0)]], state, parts=(1,))
     az3, ax3, state = hold((az3, ax3, state))
     a4 = send(az3, swap)
     state = kernel(m3, [[(az3, 0), (ax3, 0)], None], state, parts=(0,))

time: 91.8 us -> 89.9 us (0.979)
  the two profiles are of different devices: /device:TPU:29 before, /device:TPU:24 now
where the time goes in v2:
time: 89.9 us; the launch traced here: 91.4 us
  Pallas kernels  70.6 us (79%)
  starting transfers between devices  16.1 us (18%)
  local copies, waits for them, and re-layouts  3.25 us (4%)
    pallas_call x9, Pallas kernels, levels(): pl.pallas_call(partial(attend, stride, moves, fold, [[block for _, block...  70.6 us
    ppermute x14, starting transfers between devices, send(): return lax.ppermute(x, 'tp', full)  16.1 us
    unnamed x2, local copies, waits for them, and re-layouts  2.19 us
  transfers between devices with their start and end apart: 14, of which 1 were waited for; matrix products, arithmetic and copies ran while one was open for 1% of the time, Pallas kernels for 51%

profile of v2, /device:TPU:24, one launch (start us, length us, event | category | flops | bytes accessed | tf_op | source)
XLA Modules:
  0.0 91.4 jit_solution(7249756732993415761)
XLA Ops:
  0.0 1.1 %fusion = (bf16[128,1024]{1,0:T(8,128)(2,1)S(1)}, bf16[128,1024]{1,0:T(8,128)(2,1)S(1)}) fusion(bf16[128,2048]{1,0:T(8,128)(2,1)} %param.5), kind=kLoop, calls=%fused_computation.1 | loop fusion | bytes 1048576 | tf_op jit(solution)/shard_map/slice | solution.py:324
  1.1 1.7 %collective-permute-start.3 = (bf16[128,1024]{1,0:T(8,128)(2,1)S(1)}, bf16[128,1024]{1,0:T(8,128)(2,1)S(1)}, u32[]{:S(2)}, u32[]{:S(2)}) collective-permute-start(bf16[128,1024]{1,0:T(8,128)(2,1)S(1)} %get-tuple-element.81.refs_1_.refs_2_), channel_id=1, source_target_pairs={{0,2},{1,3},{2,0},{3,1},{4,6},{5,7},{6,4},{7,5},{8,10},{9,11},{10,... | collective-permute-start | bytes 786440 | tf_op jit(solution)/shard_map/ppermute | solution.py:304
  2.8 1.6 %collective-permute-start = (bf16[128,1024]{1,0:T(8,128)(2,1)S(1)}, bf16[128,1024]{1,0:T(8,128)(2,1)S(1)}, u32[]{:S(2)}, u32[]{:S(2)}) collective-permute-start(bf16[128,1024]{1,0:T(8,128)(2,1)S(1)} %get-tuple-element.82.refs_1_.refs_2_), channel_id=1, source_target_pairs={{0,4},{1,5},{2,6},{3,7},{4,8},{5,9},{6,10},{7,11},{8,12},{9,13},{1... | collective-permute-start | bytes 786440 | tf_op jit(solution)/shard_map/ppermute | solution.py:304
  4.4 0.5 collective-permute-start.1
  4.9 0.7 pad_add_fusion.table_ref
  5.7 2.2 %copy-done = bf16[128,16384]{1,0:T(8,128)(2,1)S(1)} copy-done((bf16[128,16384]{1,0:T(8,128)(2,1)S(1)}, bf16[128,16384]{1,0:T(8,128)(2,1)}, u32[]{:S(2)}) %copy-start) | copy-done | bytes 4194328
  7.9 2.6 %levels_1_first.2 = (bf16[4,128,2048]{2,1,0:T(8,128)(2,1)S(1)}, f32[4,136,2048]{2,1,0:T(8,128)S(1)}) custom-call(s32[33]{0:T(128)S(1)} %pad_add_fusion.table_ref, bf16[128,16384]{1,0:T(8,128)(2,1)S(1)} %copy-done, bf16[128,1024]{1,0:T(8,128)(2,1)S(1)} %get-tuple-element.81.refs_1_.refs_2_), custom_call_target="tpu_custom_call" | custom-call | flops 536870912 | bytes 2097152 | tf_op jit(solution)/shard_map/levels_1_first/pallas_call | solution.py:262
  10.6 1.6 %collective-permute-start.6 = (bf16[128,1024]{1,0:T(8,128)(2,1)S(1)}, bf16[128,1024]{1,0:T(8,128)(2,1)S(1)}, u32[]{:S(2)}, u32[]{:S(2)}) collective-permute-start(bf16[128,1024]{1,0:T(8,128)(2,1)S(1)} %collective-permute-done.2.refs_2_.refs_3_), channel_id=1, source_target_pairs={{0,4},{1,5},{2,6},{3,7},{4,8},{5,9},{6,10},{7,11},{8,12},{9,13},{1... | collective-permute-start | bytes 786440 | tf_op jit(solution)/shard_map/ppermute | solution.py:304
  12.2 1.7 %collective-permute-start.7 = (bf16[128,1024]{1,0:T(8,128)(2,1)S(1)}, bf16[128,1024]{1,0:T(8,128)(2,1)S(1)}, u32[]{:S(2)}, u32[]{:S(2)}) collective-permute-start(bf16[128,1024]{1,0:T(8,128)(2,1)S(1)} %collective-permute-done.2.refs_2_.refs_3_), channel_id=1, source_target_pairs={{0,2},{1,3},{2,0},{3,1},{4,6},{5,7},{6,4},{7,5},{8,10},{9,11},{10,... | collective-permute-start | bytes 786440 | tf_op jit(solution)/shard_map/ppermute | solution.py:304
  13.8 2.6 %levels_1_first.3 = (bf16[4,128,2048]{2,1,0:T(8,128)(2,1)S(1)}, f32[4,136,2048]{2,1,0:T(8,128)S(1)}) custom-call(s32[33]{0:T(128)S(1)} %pad_add_fusion.table_ref, bf16[128,16384]{1,0:T(8,128)(2,1)S(1)} %copy-done, bf16[128,1024]{1,0:T(8,128)(2,1)S(1)} %get-tuple-element.82.refs_1_.refs_2_), custom_call_target="tpu_custom_call" | custom-call | flops 536870912 | bytes 2097152 | tf_op jit(solution)/shard_map/levels_1_first/pallas_call | solution.py:262
  16.5 1.3 %collective-permute-start.4 = (bf16[128,1024]{1,0:T(8,128)(2,1)S(1)}, bf16[128,1024]{1,0:T(8,128)(2,1)S(1)}, u32[]{:S(2)}, u32[]{:S(2)}) collective-permute-start(bf16[128,1024]{1,0:T(8,128)(2,1)S(1)} %collective-permute-done.refs_2_.refs_3_), channel_id=1, source_target_pairs={{0,4},{1,5},{2,6},{3,7},{4,8},{5,9},{6,10},{7,11},{8,12},{9,13},{1... | collective-permute-start | bytes 786440 | tf_op jit(solution)/shard_map/ppermute | solution.py:304
  17.8 1.7 %collective-permute-start.5 = (bf16[128,1024]{1,0:T(8,128)(2,1)S(1)}, bf16[128,1024]{1,0:T(8,128)(2,1)S(1)}, u32[]{:S(2)}, u32[]{:S(2)}) collective-permute-start(bf16[128,1024]{1,0:T(8,128)(2,1)S(1)} %collective-permute-done.refs_2_.refs_3_), channel_id=1, source_target_pairs={{0,2},{1,3},{2,0},{3,1},{4,6},{5,7},{6,4},{7,5},{8,10},{9,11},{10,... | collective-permute-start | bytes 786440 | tf_op jit(solution)/shard_map/ppermute | solution.py:304
  19.4 3.1 %levels_2.4.refs_1_ = f32[4,136,2048]{2,1,0:T(8,128)S(1)} custom-call(s32[33]{0:T(128)S(1)} %pad_add_fusion.table_ref, bf16[4,128,2048]{2,1,0:T(8,128)(2,1)S(1)} %get-tuple-element.79.refs_0_, f32[4,136,2048]{2,1,0:T(8,128)S(1)} %get-tuple-element.52.refs_1_, bf16[128,1024]{1,0:T(8,128)(2,1)S(1)} %collective-permute-done.2.refs_2_.refs_3_, ...), custom_call_target="tpu_custom_call" | custom-call | flops 1073741824 | bytes 2097152 | tf_op jit(solution)/shard_map/levels_2/pallas_call | solution.py:262
  22.6 1.5 %collective-permute-start.10 = (bf16[128,1024]{1,0:T(8,128)(2,1)S(1)}, bf16[128,1024]{1,0:T(8,128)(2,1)S(1)}, u32[]{:S(2)}, u32[]{:S(2)}) collective-permute-start(bf16[128,1024]{1,0:T(8,128)(2,1)S(1)} %collective-permute-done.6.refs_2_.refs_5_), channel_id=1, source_target_pairs={{8,12},{9,13},{10,14},{11,15},{24,28},{25,29},{26,30},{27,31}} | collective-permute-start | bytes 786440 | tf_op jit(solution)/shard_map/ppermute | solution.py:304
  24.1 0.7 collective-permute-start.11
  24.8 3.1 %levels_2.5.refs_1_ = f32[4,136,2048]{2,1,0:T(8,128)S(1)} custom-call(s32[33]{0:T(128)S(1)} %pad_add_fusion.table_ref, bf16[4,128,2048]{2,1,0:T(8,128)(2,1)S(1)} %get-tuple-element.79.refs_0_, f32[4,136,2048]{2,1,0:T(8,128)S(1)} %levels_2.4.refs_1_, bf16[128,1024]{1,0:T(8,128)(2,1)S(1)} %collective-permute-done.6.refs_2_.refs_5_, ...), custom_call_target="tpu_custom_call" | custom-call | flops 1073741824 | bytes 2097152 | tf_op jit(solution)/shard_map/levels_2/pallas_call | solution.py:262
  28.0 1.3 %collective-permute-start.8 = (bf16[128,1024]{1,0:T(8,128)(2,1)S(1)}, bf16[128,1024]{1,0:T(8,128)(2,1)S(1)}, u32[]{:S(2)}, u32[]{:S(2)}) collective-permute-start(bf16[128,1024]{1,0:T(8,128)(2,1)S(1)} %collective-permute-done.4.refs_4_.refs_5_), channel_id=1, source_target_pairs={{8,12},{9,13},{10,14},{11,15},{24,28},{25,29},{26,30},{27,31}} | collective-permute-start | bytes 786440 | tf_op jit(solution)/shard_map/ppermute | solution.py:304
  29.3 1.0 %collective-permute-start.9 = (bf16[128,1024]{1,0:T(8,128)(2,1)S(1)}, bf16[128,1024]{1,0:T(8,128)(2,1)S(1)}, u32[]{:S(2)}, u32[]{:S(2)}) collective-permute-start(bf16[128,1024]{1,0:T(8,128)(2,1)S(1)} %collective-permute-done.4.refs_4_.refs_5_), channel_id=1, source_target_pairs={{0,2},{1,3},{2,0},{3,1},{4,6},{5,7},{6,4},{7,5},{8,10},{9,11},{10,... | collective-permute-start | bytes 786440 | tf_op jit(solution)/shard_map/ppermute | solution.py:304
  30.3 5.1 %levels_4.1.refs_1_ = f32[4,136,2048]{2,1,0:T(8,128)S(1)} custom-call(s32[33]{0:T(128)S(1)} %pad_add_fusion.table_ref, bf16[4,128,2048]{2,1,0:T(8,128)(2,1)S(1)} %get-tuple-element.75.refs_0_, f32[4,136,2048]{2,1,0:T(8,128)S(1)} %get-tuple-element.66.refs_1_, bf16[128,1024]{1,0:T(8,128)(2,1)S(1)} %collective-permute-done.refs_2_.refs_3_, ...), custom_call_target="tpu_custom_call" | custom-call | flops 2147483648 | bytes 2097152 | tf_op jit(solution)/shard_map/levels_4/pallas_call | solution.py:262
  35.4 3.1 %levels_2.6.refs_1_ = f32[4,136,2048]{2,1,0:T(8,128)S(1)} custom-call(s32[33]{0:T(128)S(1)} %pad_add_fusion.table_ref, bf16[4,128,2048]{2,1,0:T(8,128)(2,1)S(1)} %get-tuple-element.79.refs_0_, f32[4,136,2048]{2,1,0:T(8,128)S(1)} %levels_2.5.refs_1_, bf16[128,1024]{1,0:T(8,128)(2,1)S(1)} %collective-permute-done.10.refs_2_.refs_7_, ...), custom_call_target="tpu_custom_call" | custom-call | flops 1073741824 | bytes 2097152 | tf_op jit(solution)/shard_map/levels_2/pallas_call | solution.py:262
  39.0 1.5 %collective-permute-start.12 = (bf16[128,1024]{1,0:T(8,128)(2,1)S(1)}, bf16[128,1024]{1,0:T(8,128)(2,1)S(1)}, u32[]{:S(2)}, u32[]{:S(2)}) collective-permute-start(bf16[128,1024]{1,0:T(8,128)(2,1)S(1)} %collective-permute-done.9.refs_3_.refs_8_), channel_id=1, source_target_pairs={{8,12},{9,13},{10,14},{11,15},{24,28},{25,29},{26,30},{27,31}} | collective-permute-start | bytes 786440 | tf_op jit(solution)/shard_map/ppermute | solution.py:304
  40.5 3.1 %levels_2.7.refs_1_ = f32[4,136,2048]{2,1,0:T(8,128)S(1)} custom-call(s32[33]{0:T(128)S(1)} %pad_add_fusion.table_ref, bf16[4,128,2048]{2,1,0:T(8,128)(2,1)S(1)} %get-tuple-element.75.refs_0_, f32[4,136,2048]{2,1,0:T(8,128)S(1)} %levels_4.1.refs_1_, bf16[128,1024]{1,0:T(8,128)(2,1)S(1)} %collective-permute-done.8.refs_2_.refs_7_, ...), custom_call_target="tpu_custom_call" | custom-call | flops 1073741824 | bytes 2097152 | tf_op jit(solution)/shard_map/levels_2/pallas_call | solution.py:262
  43.7 23.7 %levels_1_last.2.refs_10_ = bf16[128,16384]{1,0:T(8,128)(2,1)} custom-call(s32[33]{0:T(128)S(1)} %pad_add_fusion.table_ref, bf16[4,128,2048]{2,1,0:T(8,128)(2,1)S(1)} %get-tuple-element.79.refs_0_, f32[4,136,2048]{2,1,0:T(8,128)S(1)} %levels_2.6.refs_1_, bf16[128,1024]{1,0:T(8,128)(2,1)S(1)} %get-tuple-element.81.refs_1_.refs_2_, ...), custom_call_target="tpu_custom_call" | custom-call | flops 536870912 | bytes 2097152 | tf_op jit(solution)/shard_map/levels_1_last/pallas_call | solution.py:262
  67.4 24.0 %levels_1_last.3 = bf16[128,16384]{1,0:T(8,128)(2,1)} custom-call(s32[33]{0:T(128)S(1)} %pad_add_fusion.table_ref, bf16[4,128,2048]{2,1,0:T(8,128)(2,1)S(1)} %get-tuple-element.75.refs_0_, f32[4,136,2048]{2,1,0:T(8,128)S(1)} %levels_2.7.refs_1_, bf16[128,1024]{1,0:T(8,128)(2,1)S(1)} %get-tuple-element.82.refs_1_.refs_2_, ...), custom_call_target="tpu_custom_call", output_to_operand_aliasing={{}: (11, {})} | custom-call | flops 536870912 | bytes 2097152 | tf_op jit(solution)/shard_map/levels_1_last/pallas_call | solution.py:262
  (17 shorter events, 0.6 us)
Async XLA Ops:
  1.1 9.5 %collective-permute-start.2 = (bf16[128,1024]{1,0:T(8,128)(2,1)S(1)}, bf16[128,1024]{1,0:T(8,128)(2,1)S(1)}, u32[]{:S(2)}, u32[]{:S(2)}) collective-permute-start(bf16[128,1024]{1,0:T(8,128)(2,1)S(1)} %get-tuple-element.81.refs_1_.refs_2_), channel_id=1, source_target_pairs={{0,4},{1,5},{2,6},{3,7},{4,8},{5,9},{6,10},{7,11},{8,12},{9,13},{1... | collective-permute-start | bytes 786440 | tf_op jit(solution)/shard_map/ppermute | solution.py:304
  1.1 9.4 %collective-permute-start.3 = (bf16[128,1024]{1,0:T(8,128)(2,1)S(1)}, bf16[128,1024]{1,0:T(8,128)(2,1)S(1)}, u32[]{:S(2)}, u32[]{:S(2)}) collective-permute-start(bf16[128,1024]{1,0:T(8,128)(2,1)S(1)} %get-tuple-element.81.refs_1_.refs_2_), channel_id=1, source_target_pairs={{0,2},{1,3},{2,0},{3,1},{4,6},{5,7},{6,4},{7,5},{8,10},{9,11},{10,... | collective-permute-start | bytes 786440 | tf_op jit(solution)/shard_map/ppermute | solution.py:304
  2.8 13.6 %collective-permute-start = (bf16[128,1024]{1,0:T(8,128)(2,1)S(1)}, bf16[128,1024]{1,0:T(8,128)(2,1)S(1)}, u32[]{:S(2)}, u32[]{:S(2)}) collective-permute-start(bf16[128,1024]{1,0:T(8,128)(2,1)S(1)} %get-tuple-element.82.refs_1_.refs_2_), channel_id=1, source_target_pairs={{0,4},{1,5},{2,6},{3,7},{4,8},{5,9},{6,10},{7,11},{8,12},{9,13},{1... | collective-permute-start | bytes 786440 | tf_op jit(solution)/shard_map/ppermute | solution.py:304
  4.4 12.1 %collective-permute-start.1 = (bf16[128,1024]{1,0:T(8,128)(2,1)S(1)}, bf16[128,1024]{1,0:T(8,128)(2,1)S(1)}, u32[]{:S(2)}, u32[]{:S(2)}) collective-permute-start(bf16[128,1024]{1,0:T(8,128)(2,1)S(1)} %get-tuple-element.82.refs_1_.refs_2_), channel_id=1, source_target_pairs={{0,2},{1,3},{2,0},{3,1},{4,6},{5,7},{6,4},{7,5},{8,10},{9,11},{10,... | collective-permute-start | bytes 786440 | tf_op jit(solution)/shard_map/ppermute | solution.py:304
  5.7 2.2 %copy-start = (bf16[128,16384]{1,0:T(8,128)(2,1)S(1)}, bf16[128,16384]{1,0:T(8,128)(2,1)}, u32[]{:S(2)}) copy-start(bf16[128,16384]{1,0:T(8,128)(2,1)} %refs_0_.3) | copy-start | bytes 12582916
  10.6 12.0 %collective-permute-start.6 = (bf16[128,1024]{1,0:T(8,128)(2,1)S(1)}, bf16[128,1024]{1,0:T(8,128)(2,1)S(1)}, u32[]{:S(2)}, u32[]{:S(2)}) collective-permute-start(bf16[128,1024]{1,0:T(8,128)(2,1)S(1)} %collective-permute-done.2.refs_2_.refs_3_), channel_id=1, source_target_pairs={{0,4},{1,5},{2,6},{3,7},{4,8},{5,9},{6,10},{7,11},{8,12},{9,13},{1... | collective-permute-start | bytes 786440 | tf_op jit(solution)/shard_map/ppermute | solution.py:304
  12.2 10.4 %collective-permute-start.7 = (bf16[128,1024]{1,0:T(8,128)(2,1)S(1)}, bf16[128,1024]{1,0:T(8,128)(2,1)S(1)}, u32[]{:S(2)}, u32[]{:S(2)}) collective-permute-start(bf16[128,1024]{1,0:T(8,128)(2,1)S(1)} %collective-permute-done.2.refs_2_.refs_3_), channel_id=1, source_target_pairs={{0,2},{1,3},{2,0},{3,1},{4,6},{5,7},{6,4},{7,5},{8,10},{9,11},{10,... | collective-permute-start | bytes 786440 | tf_op jit(solution)/shard_map/ppermute | solution.py:304
  16.5 11.5 %collective-permute-start.4 = (bf16[128,1024]{1,0:T(8,128)(2,1)S(1)}, bf16[128,1024]{1,0:T(8,128)(2,1)S(1)}, u32[]{:S(2)}, u32[]{:S(2)}) collective-permute-start(bf16[128,1024]{1,0:T(8,128)(2,1)S(1)} %collective-permute-done.refs_2_.refs_3_), channel_id=1, source_target_pairs={{0,4},{1,5},{2,6},{3,7},{4,8},{5,9},{6,10},{7,11},{8,12},{9,13},{1... | collective-permute-start | bytes 786440 | tf_op jit(solution)/shard_map/ppermute | solution.py:304
  17.8 10.2 %collective-permute-start.5 = (bf16[128,1024]{1,0:T(8,128)(2,1)S(1)}, bf16[128,1024]{1,0:T(8,128)(2,1)S(1)}, u32[]{:S(2)}, u32[]{:S(2)}) collective-permute-start(bf16[128,1024]{1,0:T(8,128)(2,1)S(1)} %collective-permute-done.refs_2_.refs_3_), channel_id=1, source_target_pairs={{0,2},{1,3},{2,0},{3,1},{4,6},{5,7},{6,4},{7,5},{8,10},{9,11},{10,... | collective-permute-start | bytes 786440 | tf_op jit(solution)/shard_map/ppermute | solution.py:304
  22.6 12.8 %collective-permute-start.10 = (bf16[128,1024]{1,0:T(8,128)(2,1)S(1)}, bf16[128,1024]{1,0:T(8,128)(2,1)S(1)}, u32[]{:S(2)}, u32[]{:S(2)}) collective-permute-start(bf16[128,1024]{1,0:T(8,128)(2,1)S(1)} %collective-permute-done.6.refs_2_.refs_5_), channel_id=1, source_target_pairs={{8,12},{9,13},{10,14},{11,15},{24,28},{25,29},{26,30},{27,31}} | collective-permute-start | bytes 786440 | tf_op jit(solution)/shard_map/ppermute | solution.py:304
  24.1 11.3 %collective-permute-start.11 = (bf16[128,1024]{1,0:T(8,128)(2,1)S(1)}, bf16[128,1024]{1,0:T(8,128)(2,1)S(1)}, u32[]{:S(2)}, u32[]{:S(2)}) collective-permute-start(bf16[128,1024]{1,0:T(8,128)(2,1)S(1)} %collective-permute-done.6.refs_2_.refs_5_), channel_id=1, source_target_pairs={{0,2},{1,3},{2,0},{3,1},{4,6},{5,7},{6,4},{7,5},{8,10},{9,11},{10,... | collective-permute-start | bytes 786440 | tf_op jit(solution)/shard_map/ppermute | solution.py:304
  28.0 10.6 %collective-permute-start.8 = (bf16[128,1024]{1,0:T(8,128)(2,1)S(1)}, bf16[128,1024]{1,0:T(8,128)(2,1)S(1)}, u32[]{:S(2)}, u32[]{:S(2)}) collective-permute-start(bf16[128,1024]{1,0:T(8,128)(2,1)S(1)} %collective-permute-done.4.refs_4_.refs_5_), channel_id=1, source_target_pairs={{8,12},{9,13},{10,14},{11,15},{24,28},{25,29},{26,30},{27,31}} | collective-permute-start | bytes 786440 | tf_op jit(solution)/shard_map/ppermute | solution.py:304
  29.3 9.7 %collective-permute-start.9 = (bf16[128,1024]{1,0:T(8,128)(2,1)S(1)}, bf16[128,1024]{1,0:T(8,128)(2,1)S(1)}, u32[]{:S(2)}, u32[]{:S(2)}) collective-permute-start(bf16[128,1024]{1,0:T(8,128)(2,1)S(1)} %collective-permute-done.4.refs_4_.refs_5_), channel_id=1, source_target_pairs={{0,2},{1,3},{2,0},{3,1},{4,6},{5,7},{6,4},{7,5},{8,10},{9,11},{10,... | collective-permute-start | bytes 786440 | tf_op jit(solution)/shard_map/ppermute | solution.py:304
  35.4 8.3 %collective-permute-start.13 = (bf16[128,1024]{1,0:T(8,128)(2,1)S(1)}, bf16[128,1024]{1,0:T(8,128)(2,1)S(1)}, u32[]{:S(2)}, u32[]{:S(2)}) collective-permute-start(bf16[128,1024]{1,0:T(8,128)(2,1)S(1)} %collective-permute-done.10.refs_2_.refs_7_), channel_id=1, source_target_pairs={{0,2},{1,3},{2,0},{3,1},{4,6},{5,7},{6,4},{7,5},{8,10},{9,11},{10,... | collective-permute-start | bytes 786440 | tf_op jit(solution)/shard_map/ppermute | solution.py:304
  39.0 28.4 %collective-permute-start.12 = (bf16[128,1024]{1,0:T(8,128)(2,1)S(1)}, bf16[128,1024]{1,0:T(8,128)(2,1)S(1)}, u32[]{:S(2)}, u32[]{:S(2)}) collective-permute-start(bf16[128,1024]{1,0:T(8,128)(2,1)S(1)} %collective-permute-done.9.refs_3_.refs_8_), channel_id=1, source_target_pairs={{8,12},{9,13},{10,14},{11,15},{24,28},{25,29},{26,30},{27,31}} | collective-permute-start | bytes 786440 | tf_op jit(solution)/shard_map/ppermute | solution.py:304

commit v3 on v2

--- a/solution.py
+++ b/solution.py
@@ -73,7 +73,9 @@
         if first:
             qt_refs = [refs.pop(0) for _ in parts]
         new_refs = [refs.pop(0) for _ in parts]
-    k_buf, v_buf, bad_buf = refs
+    k_buf, v_buf, bad_buf = refs[:3]
+    if last:
+        out_buf, sems = refs[3:]
 
     me = table_ref[0]
     count = count_of(table_ref, me)
@@ -138,8 +140,16 @@
         for u in range(k):
             for g in range(group):
                 at = u * lanes + g * TILE
-                to = (h * group + g) * HD
-                out_ref[down(t + u), to:to + HD] = result[at:at + TILE]
+                to = pl.multiple_of((head + h) * group * HD + g * HD, HD)
+                out_buf[down(t + u), pl.ds(to, HD)] = result[at:at + TILE]
+
+    def leave(h):
+        size = group * HD
+        return pltpu.make_async_copy(
+            out_buf.at[:, pl.ds(pl.multiple_of(h * size, size), size)],
+            out_ref.at[:, pl.ds(pl.multiple_of((parts[0] * held + h) * size, size), size)],
+            sems.at[h],
+        )
 
     def unshifted(i, h, t, k, s):
         w = jnp.exp2(s * FACTOR)
@@ -153,7 +163,7 @@
         if last:
             total = mixed[TOTAL:TOTAL + 1]
             good = (total >= SMALLEST) & (total <= LARGEST)
-            bad_buf[h:h + 1, across(t, k)] = jnp.where(good, 0.0, 1.0)
+            bad_buf[pl.ds(head + h, 1), across(t, k)] = jnp.where(good, 0.0, 1.0)
             write(h, t, k, mixed[:HD], total)
         else:
             new_refs[i][head + h, :, across(t, k)] = mixed
@@ -163,8 +173,9 @@
             mixed = old_refs[i][head + h, :, across(0, k)]
             total = mixed[TOTAL:TOTAL + 1]
             good = (total >= SMALLEST) & (total <= LARGEST)
-            bad_buf[h:h + 1, across(0, k)] = jnp.where(good, 0.0, 1.0)
+            bad_buf[pl.ds(head + h, 1), across(0, k)] = jnp.where(good, 0.0, 1.0)
             write(h, 0, k, mixed[:HD], total)
+            leave(head + h).start()
 
     def run(i, k):
         units = [(i, h, t, min(UNIT, k - t)) for h in range(STEP) for t in range(0, k, UNIT)]
@@ -172,6 +183,8 @@
         for at, unit in enumerate(units):
             following = scores(*units[at + 1]) if at + 1 < len(units) else None
             unshifted(*unit, s)
+            if last and (at + 1 == len(units) or units[at + 1][1] != unit[1]):
+                leave(head + unit[1]).start()
             s = following
 
     def shifted(i, h, t, _):
@@ -198,12 +211,26 @@
         return 0
 
     def safely(i):
-        for h in range(STEP):
-            lax.fori_loop(0, tiles, partial(shifted, i, h), 0)
+        def again(h, _):
+            leave(h).wait()
+            lax.fori_loop(0, tiles, partial(shifted, i, h - head), 0)
+            leave(h).start()
+            return 0
+
+        lax.fori_loop(0, held, again, 0)
 
     def keep(i):
         for h in range(STEP):
             new_refs[i][head + h] = old_refs[i][head + h]
+
+    if last:
+        def clear(t, _):
+            size = STEP * group * HD
+            part = pl.ds(pl.multiple_of(head * group * HD, size), size)
+            out_buf[down(t), part] = jnp.zeros((TILE, size), out_buf.dtype)
+            return 0
+
+        lax.fori_loop(tiles, tiles_max, clear, 0)
 
     some = sum(lengths.values()) > 0
     for i in range(many):
@@ -211,22 +238,27 @@
         mine = here & some
         pl.when(mine)(partial(fill, i))
         if last:
-            bad_buf[...] = jnp.zeros(bad_buf.shape, jnp.float32)
+            @pl.when(pl.program_id(0) == 0)
+            def _():
+                bad_buf[...] = jnp.zeros(bad_buf.shape, jnp.float32)
+
         for k in range(1, tiles_max + 1):
             pl.when(mine & (tiles == k))(partial(run, i, k))
             if last:
                 pl.when(here & jnp.logical_not(some) & (tiles == k))(partial(settle, i, k))
         if last:
-            pl.when(here & (jnp.max(bad_buf[:STEP, :]) > 0.0))(partial(safely, i))
+            @pl.when(pl.program_id(0) == steps - 1)
+            def _():
+                pl.when(here & (jnp.max(bad_buf[...]) > 0.0))(partial(safely, i))
+
         elif not first:
             pl.when(here & jnp.logical_not(some))(partial(keep, i))
 
     if last:
-        def clear(t, _):
-            out_ref[down(t), :] = jnp.zeros((TILE, out_ref.shape[1]), out_ref.dtype)
-            return 0
-
-        lax.fori_loop(tiles, tiles_max, clear, 0)
+        @pl.when(pl.program_id(0) == steps - 1)
+        def _():
+            for h in range(held):
+                leave(h).wait()
 
 
 def levels(stride, table, queries, kv_heads, moves, kvs, state, parts=(0, 1), fold=None, last=False, into=None, begin=False):
@@ -251,8 +283,10 @@
         specs.append(pl.BlockSpec(memory_space=pl.ANY))
         aliases = {1 + len(operands): 0}
         operands.append(into)
-    if last:
-        out_specs = pl.BlockSpec((rows, STEP * group * HD), lambda k, *_: (0, k + parts[0] * steps))
+    extra = []
+    if last:
+        extra = [pltpu.VMEM((rows, half * group * HD), jnp.bfloat16), pltpu.SemaphoreType.DMA((half,))]
+        out_specs = pl.BlockSpec(memory_space=pl.ANY)
         out_shape = jax.ShapeDtypeStruct((rows, width), jnp.bfloat16)
     else:
         turned = jax.ShapeDtypeStruct((half, HD, tiles_max * lanes), jnp.bfloat16)
@@ -270,7 +304,7 @@
                 pltpu.VMEM((STEP, n * rows, HD), jnp.bfloat16),
                 pltpu.VMEM((STEP, VROWS, n * rows), jnp.bfloat16),
                 pltpu.VMEM((8, tiles_max * lanes), jnp.float32),
-            ],
+            ] + extra,
         ),
         out_shape=out_shape,
         input_output_aliases=aliases,

time: 89.9 us -> 91.7 us (1.020)
  the two profiles are of different devices: /device:TPU:24 before, /device:TPU:26 now
where the time goes in v3:
time: 91.7 us; the launch traced here: 90.6 us
  Pallas kernels  64 us (70%)
  starting transfers between devices  15 us (16%)
  waiting for transfers between devices  7.27 us (8%)
  local copies, waits for them, and re-layouts  3.25 us (4%)
    pallas_call x9, Pallas kernels, levels(): pl.pallas_call(partial(attend, stride, moves, fold, [[block for _, block...  64 us
    ppermute x14, starting transfers between devices, send(): return lax.ppermute(x, 'tp', full)  15 us
    ppermute x14, waiting for transfers between devices, send(): return lax.ppermute(x, 'tp', full)  7.27 us
    unnamed x2, local copies, waits for them, and re-layouts  2.19 us
  transfers between devices with their start and end apart: 14, of which 9 were waited for; matrix products, arithmetic and copies ran while one was open for 1% of the time, Pallas kernels for 44%

profile of v3, /device:TPU:26, one launch (start us, length us, event | category | flops | bytes accessed | tf_op | source)
XLA Modules:
  0.0 90.6 jit_solution(7012812285753398104)
XLA Ops:
  0.0 1.1 %fusion = (bf16[128,1024]{1,0:T(8,128)(2,1)S(1)}, bf16[128,1024]{1,0:T(8,128)(2,1)S(1)}) fusion(bf16[128,2048]{1,0:T(8,128)(2,1)} %param.5), kind=kLoop, calls=%fused_computation.1 | loop fusion | bytes 1048576 | tf_op jit(solution)/shard_map/slice | solution.py:358
  1.7 1.7 %collective-permute-start = (bf16[128,1024]{1,0:T(8,128)(2,1)S(1)}, bf16[128,1024]{1,0:T(8,128)(2,1)S(1)}, u32[]{:S(2)}, u32[]{:S(2)}) collective-permute-start(bf16[128,1024]{1,0:T(8,128)(2,1)S(1)} %get-tuple-element.82.refs_1_.refs_2_), channel_id=1, source_target_pairs={{0,4},{1,5},{2,6},{3,7},{4,8},{5,9},{6,10},{7,11},{8,12},{9,13},{1... | collective-permute-start | bytes 786440 | tf_op jit(solution)/shard_map/ppermute | solution.py:338
  3.5 1.5 %collective-permute-start.1 = (bf16[128,1024]{1,0:T(8,128)(2,1)S(1)}, bf16[128,1024]{1,0:T(8,128)(2,1)S(1)}, u32[]{:S(2)}, u32[]{:S(2)}) collective-permute-start(bf16[128,1024]{1,0:T(8,128)(2,1)S(1)} %get-tuple-element.82.refs_1_.refs_2_), channel_id=1, source_target_pairs={{0,2},{1,3},{2,0},{3,1},{4,6},{5,7},{6,4},{7,5},{8,10},{9,11},{10,... | collective-permute-start | bytes 786440 | tf_op jit(solution)/shard_map/ppermute | solution.py:338
  4.9 0.7 pad_add_fusion.table_ref
  5.7 2.2 %copy-done = bf16[128,16384]{1,0:T(8,128)(2,1)S(1)} copy-done((bf16[128,16384]{1,0:T(8,128)(2,1)S(1)}, bf16[128,16384]{1,0:T(8,128)(2,1)}, u32[]{:S(2)}) %copy-start) | copy-done | bytes 4194328
  7.9 2.6 %levels_1_first.2 = (bf16[4,128,2048]{2,1,0:T(8,128)(2,1)S(1)}, f32[4,136,2048]{2,1,0:T(8,128)S(1)}) custom-call(s32[33]{0:T(128)S(1)} %pad_add_fusion.table_ref, bf16[128,16384]{1,0:T(8,128)(2,1)S(1)} %copy-done, bf16[128,1024]{1,0:T(8,128)(2,1)S(1)} %get-tuple-element.81.refs_1_.refs_2_), custom_call_target="tpu_custom_call" | custom-call | flops 536870912 | bytes 2097152 | tf_op jit(solution)/shard_map/levels_1_first/pallas_call | solution.py:296
  10.6 1.8 %collective-permute-start.6 = (bf16[128,1024]{1,0:T(8,128)(2,1)S(1)}, bf16[128,1024]{1,0:T(8,128)(2,1)S(1)}, u32[]{:S(2)}, u32[]{:S(2)}) collective-permute-start(bf16[128,1024]{1,0:T(8,128)(2,1)S(1)} %collective-permute-done.2.refs_2_.refs_3_), channel_id=1, source_target_pairs={{0,4},{1,5},{2,6},{3,7},{4,8},{5,9},{6,10},{7,11},{8,12},{9,13},{1... | collective-permute-start | bytes 786440 | tf_op jit(solution)/shard_map/ppermute | solution.py:338
  12.7 2.6 %levels_1_first.3 = (bf16[4,128,2048]{2,1,0:T(8,128)(2,1)S(1)}, f32[4,136,2048]{2,1,0:T(8,128)S(1)}) custom-call(s32[33]{0:T(128)S(1)} %pad_add_fusion.table_ref, bf16[128,16384]{1,0:T(8,128)(2,1)S(1)} %copy-done, bf16[128,1024]{1,0:T(8,128)(2,1)S(1)} %get-tuple-element.82.refs_1_.refs_2_), custom_call_target="tpu_custom_call" | custom-call | flops 536870912 | bytes 2097152 | tf_op jit(solution)/shard_map/levels_1_first/pallas_call | solution.py:296
  16.2 1.8 %collective-permute-start.4 = (bf16[128,1024]{1,0:T(8,128)(2,1)S(1)}, bf16[128,1024]{1,0:T(8,128)(2,1)S(1)}, u32[]{:S(2)}, u32[]{:S(2)}) collective-permute-start(bf16[128,1024]{1,0:T(8,128)(2,1)S(1)} %collective-permute-done.refs_2_.refs_3_), channel_id=1, source_target_pairs={{0,4},{1,5},{2,6},{3,7},{4,8},{5,9},{6,10},{7,11},{8,12},{9,13},{1... | collective-permute-start | bytes 786440 | tf_op jit(solution)/shard_map/ppermute | solution.py:338
  18.3 1.0 %levels_2.4.refs_1_ = f32[4,136,2048]{2,1,0:T(8,128)S(1)} custom-call(s32[33]{0:T(128)S(1)} %pad_add_fusion.table_ref, bf16[4,128,2048]{2,1,0:T(8,128)(2,1)S(1)} %get-tuple-element.79.refs_0_, f32[4,136,2048]{2,1,0:T(8,128)S(1)} %get-tuple-element.52.refs_1_, bf16[128,1024]{1,0:T(8,128)(2,1)S(1)} %collective-permute-done.2.refs_2_.refs_3_, ...), custom_call_target="tpu_custom_call" | custom-call | flops 1073741824 | bytes 2097152 | tf_op jit(solution)/shard_map/levels_2/pallas_call | solution.py:296
  19.3 2.2 %collective-permute-done.6.refs_2_.refs_5_ = bf16[128,1024]{1,0:T(8,128)(2,1)S(1)} collective-permute-done((bf16[128,1024]{1,0:T(8,128)(2,1)S(1)}, bf16[128,1024]{1,0:T(8,128)(2,1)S(1)}, u32[]{:S(2)}, u32[]{:S(2)}) %collective-permute-start.6) | collective-permute-done | bytes 262176 | tf_op jit(solution)/shard_map/ppermute | solution.py:338
  21.8 1.5 %collective-permute-start.10 = (bf16[128,1024]{1,0:T(8,128)(2,1)S(1)}, bf16[128,1024]{1,0:T(8,128)(2,1)S(1)}, u32[]{:S(2)}, u32[]{:S(2)}) collective-permute-start(bf16[128,1024]{1,0:T(8,128)(2,1)S(1)} %collective-permute-done.6.refs_2_.refs_5_), channel_id=1, source_target_pairs={{8,12},{9,13},{10,14},{11,15},{24,28},{25,29},{26,30},{27,31}} | collective-permute-start | bytes 786440 | tf_op jit(solution)/shard_map/ppermute | solution.py:338
  23.7 3.1 %levels_2.5.refs_1_ = f32[4,136,2048]{2,1,0:T(8,128)S(1)} custom-call(s32[33]{0:T(128)S(1)} %pad_add_fusion.table_ref, bf16[4,128,2048]{2,1,0:T(8,128)(2,1)S(1)} %get-tuple-element.79.refs_0_, f32[4,136,2048]{2,1,0:T(8,128)S(1)} %levels_2.4.refs_1_, bf16[128,1024]{1,0:T(8,128)(2,1)S(1)} %collective-permute-done.6.refs_2_.refs_5_, ...), custom_call_target="tpu_custom_call" | custom-call | flops 1073741824 | bytes 2097152 | tf_op jit(solution)/shard_map/levels_2/pallas_call | solution.py:296
  27.4 1.3 %collective-permute-start.8 = (bf16[128,1024]{1,0:T(8,128)(2,1)S(1)}, bf16[128,1024]{1,0:T(8,128)(2,1)S(1)}, u32[]{:S(2)}, u32[]{:S(2)}) collective-permute-start(bf16[128,1024]{1,0:T(8,128)(2,1)S(1)} %collective-permute-done.4.refs_4_.refs_5_), channel_id=1, source_target_pairs={{8,12},{9,13},{10,14},{11,15},{24,28},{25,29},{26,30},{27,31}} | collective-permute-start | bytes 786440 | tf_op jit(solution)/shard_map/ppermute | solution.py:338
  28.7 1.2 %collective-permute-start.9 = (bf16[128,1024]{1,0:T(8,128)(2,1)S(1)}, bf16[128,1024]{1,0:T(8,128)(2,1)S(1)}, u32[]{:S(2)}, u32[]{:S(2)}) collective-permute-start(bf16[128,1024]{1,0:T(8,128)(2,1)S(1)} %collective-permute-done.4.refs_4_.refs_5_), channel_id=1, source_target_pairs={{0,2},{1,3},{2,0},{3,1},{4,6},{5,7},{6,4},{7,5},{8,10},{9,11},{10,... | collective-permute-start | bytes 786440 | tf_op jit(solution)/shard_map/ppermute | solution.py:338
  29.9 5.1 %levels_4.1.refs_1_ = f32[4,136,2048]{2,1,0:T(8,128)S(1)} custom-call(s32[33]{0:T(128)S(1)} %pad_add_fusion.table_ref, bf16[4,128,2048]{2,1,0:T(8,128)(2,1)S(1)} %get-tuple-element.75.refs_0_, f32[4,136,2048]{2,1,0:T(8,128)S(1)} %get-tuple-element.66.refs_1_, bf16[128,1024]{1,0:T(8,128)(2,1)S(1)} %collective-permute-done.refs_2_.refs_3_, ...), custom_call_target="tpu_custom_call" | custom-call | flops 2147483648 | bytes 2097152 | tf_op jit(solution)/shard_map/levels_4/pallas_call | solution.py:296
  35.0 1.0 %collective-permute-start.13 = (bf16[128,1024]{1,0:T(8,128)(2,1)S(1)}, bf16[128,1024]{1,0:T(8,128)(2,1)S(1)}, u32[]{:S(2)}, u32[]{:S(2)}) collective-permute-start(bf16[128,1024]{1,0:T(8,128)(2,1)S(1)} %collective-permute-done.10.refs_2_.refs_7_), channel_id=1, source_target_pairs={{0,2},{1,3},{2,0},{3,1},{4,6},{5,7},{6,4},{7,5},{8,10},{9,11},{10,... | collective-permute-start | bytes 786440 | tf_op jit(solution)/shard_map/ppermute | solution.py:338
  36.0 1.0 %levels_2.6.refs_1_ = f32[4,136,2048]{2,1,0:T(8,128)S(1)} custom-call(s32[33]{0:T(128)S(1)} %pad_add_fusion.table_ref, bf16[4,128,2048]{2,1,0:T(8,128)(2,1)S(1)} %get-tuple-element.79.refs_0_, f32[4,136,2048]{2,1,0:T(8,128)S(1)} %levels_2.5.refs_1_, bf16[128,1024]{1,0:T(8,128)(2,1)S(1)} %collective-permute-done.10.refs_2_.refs_7_, ...), custom_call_target="tpu_custom_call" | custom-call | flops 1073741824 | bytes 2097152 | tf_op jit(solution)/shard_map/levels_2/pallas_call | solution.py:296
  37.3 1.4 %collective-permute-done.9.refs_3_.refs_8_ = bf16[128,1024]{1,0:T(8,128)(2,1)S(1)} collective-permute-done((bf16[128,1024]{1,0:T(8,128)(2,1)S(1)}, bf16[128,1024]{1,0:T(8,128)(2,1)S(1)}, u32[]{:S(2)}, u32[]{:S(2)}) %collective-permute-start.9) | collective-permute-done | bytes 262176 | tf_op jit(solution)/shard_map/ppermute | solution.py:338
  38.6 1.5 %collective-permute-start.12 = (bf16[128,1024]{1,0:T(8,128)(2,1)S(1)}, bf16[128,1024]{1,0:T(8,128)(2,1)S(1)}, u32[]{:S(2)}, u32[]{:S(2)}) collective-permute-start(bf16[128,1024]{1,0:T(8,128)(2,1)S(1)} %collective-permute-done.9.refs_3_.refs_8_), channel_id=1, source_target_pairs={{8,12},{9,13},{10,14},{11,15},{24,28},{25,29},{26,30},{27,31}} | collective-permute-start | bytes 786440 | tf_op jit(solution)/shard_map/ppermute | solution.py:338
  40.2 1.0 %levels_2.7.refs_1_ = f32[4,136,2048]{2,1,0:T(8,128)S(1)} custom-call(s32[33]{0:T(128)S(1)} %pad_add_fusion.table_ref, bf16[4,128,2048]{2,1,0:T(8,128)(2,1)S(1)} %get-tuple-element.75.refs_0_, f32[4,136,2048]{2,1,0:T(8,128)S(1)} %levels_4.1.refs_1_, bf16[128,1024]{1,0:T(8,128)(2,1)S(1)} %collective-permute-done.8.refs_2_.refs_7_, ...), custom_call_target="tpu_custom_call" | custom-call | flops 1073741824 | bytes 2097152 | tf_op jit(solution)/shard_map/levels_2/pallas_call | solution.py:296
  41.2 1.7 %collective-permute-done.13.refs_9_ = bf16[128,1024]{1,0:T(8,128)(2,1)S(1)} collective-permute-done((bf16[128,1024]{1,0:T(8,128)(2,1)S(1)}, bf16[128,1024]{1,0:T(8,128)(2,1)S(1)}, u32[]{:S(2)}, u32[]{:S(2)}) %collective-permute-start.13) | collective-permute-done | bytes 262176 | tf_op jit(solution)/shard_map/ppermute | solution.py:338
  43.0 23.6 %levels_1_last.2.refs_10_ = bf16[128,16384]{1,0:T(8,128)(2,1)} custom-call(s32[33]{0:T(128)S(1)} %pad_add_fusion.table_ref, bf16[4,128,2048]{2,1,0:T(8,128)(2,1)S(1)} %get-tuple-element.79.refs_0_, f32[4,136,2048]{2,1,0:T(8,128)S(1)} %levels_2.6.refs_1_, bf16[128,1024]{1,0:T(8,128)(2,1)S(1)} %get-tuple-element.81.refs_1_.refs_2_, ...), custom_call_target="tpu_custom_call" | custom-call | flops 536870912 | bytes 2097152 | tf_op jit(solution)/shard_map/levels_1_last/pallas_call | solution.py:296
  66.5 23.8 %levels_1_last.3 = bf16[128,16384]{1,0:T(8,128)(2,1)} custom-call(s32[33]{0:T(128)S(1)} %pad_add_fusion.table_ref, bf16[4,128,2048]{2,1,0:T(8,128)(2,1)S(1)} %get-tuple-element.75.refs_0_, f32[4,136,2048]{2,1,0:T(8,128)S(1)} %levels_2.7.refs_1_, bf16[128,1024]{1,0:T(8,128)(2,1)S(1)} %get-tuple-element.82.refs_1_.refs_2_, ...), custom_call_target="tpu_custom_call", output_to_operand_aliasing={{}: (11, {})} | custom-call | flops 536870912 | bytes 2097152 | tf_op jit(solution)/shard_map/levels_1_last/pallas_call | solution.py:296
  (17 shorter events, 3.7 us)
Async XLA Ops:
  1.1 9.5 %collective-permute-start.2 = (bf16[128,1024]{1,0:T(8,128)(2,1)S(1)}, bf16[128,1024]{1,0:T(8,128)(2,1)S(1)}, u32[]{:S(2)}, u32[]{:S(2)}) collective-permute-start(bf16[128,1024]{1,0:T(8,128)(2,1)S(1)} %get-tuple-element.81.refs_1_.refs_2_), channel_id=1, source_target_pairs={{0,4},{1,5},{2,6},{3,7},{4,8},{5,9},{6,10},{7,11},{8,12},{9,13},{1... | collective-permute-start | bytes 786440 | tf_op jit(solution)/shard_map/ppermute | solution.py:338
  1.3 9.2 %collective-permute-start.3 = (bf16[128,1024]{1,0:T(8,128)(2,1)S(1)}, bf16[128,1024]{1,0:T(8,128)(2,1)S(1)}, u32[]{:S(2)}, u32[]{:S(2)}) collective-permute-start(bf16[128,1024]{1,0:T(8,128)(2,1)S(1)} %get-tuple-element.81.refs_1_.refs_2_), channel_id=1, source_target_pairs={{0,2},{1,3},{2,0},{3,1},{4,6},{5,7},{6,4},{7,5},{8,10},{9,11},{10,... | collective-permute-start | bytes 786440 | tf_op jit(solution)/shard_map/ppermute | solution.py:338
  1.7 14.2 %collective-permute-start = (bf16[128,1024]{1,0:T(8,128)(2,1)S(1)}, bf16[128,1024]{1,0:T(8,128)(2,1)S(1)}, u32[]{:S(2)}, u32[]{:S(2)}) collective-permute-start(bf16[128,1024]{1,0:T(8,128)(2,1)S(1)} %get-tuple-element.82.refs_1_.refs_2_), channel_id=1, source_target_pairs={{0,4},{1,5},{2,6},{3,7},{4,8},{5,9},{6,10},{7,11},{8,12},{9,13},{1... | collective-permute-start | bytes 786440 | tf_op jit(solution)/shard_map/ppermute | solution.py:338
  3.5 12.7 %collective-permute-start.1 = (bf16[128,1024]{1,0:T(8,128)(2,1)S(1)}, bf16[128,1024]{1,0:T(8,128)(2,1)S(1)}, u32[]{:S(2)}, u32[]{:S(2)}) collective-permute-start(bf16[128,1024]{1,0:T(8,128)(2,1)S(1)} %get-tuple-element.82.refs_1_.refs_2_), channel_id=1, source_target_pairs={{0,2},{1,3},{2,0},{3,1},{4,6},{5,7},{6,4},{7,5},{8,10},{9,11},{10,... | collective-permute-start | bytes 786440 | tf_op jit(solution)/shard_map/ppermute | solution.py:338
  5.7 2.2 %copy-start = (bf16[128,16384]{1,0:T(8,128)(2,1)S(1)}, bf16[128,16384]{1,0:T(8,128)(2,1)}, u32[]{:S(2)}) copy-start(bf16[128,16384]{1,0:T(8,128)(2,1)} %refs_0_.3) | copy-start | bytes 12582916
  10.6 11.0 %collective-permute-start.6 = (bf16[128,1024]{1,0:T(8,128)(2,1)S(1)}, bf16[128,1024]{1,0:T(8,128)(2,1)S(1)}, u32[]{:S(2)}, u32[]{:S(2)}) collective-permute-start(bf16[128,1024]{1,0:T(8,128)(2,1)S(1)} %collective-permute-done.2.refs_2_.refs_3_), channel_id=1, source_target_pairs={{0,4},{1,5},{2,6},{3,7},{4,8},{5,9},{6,10},{7,11},{8,12},{9,13},{1... | collective-permute-start | bytes 786440 | tf_op jit(solution)/shard_map/ppermute | solution.py:338
  12.3 9.5 %collective-permute-start.7 = (bf16[128,1024]{1,0:T(8,128)(2,1)S(1)}, bf16[128,1024]{1,0:T(8,128)(2,1)S(1)}, u32[]{:S(2)}, u32[]{:S(2)}) collective-permute-start(bf16[128,1024]{1,0:T(8,128)(2,1)S(1)} %collective-permute-done.2.refs_2_.refs_3_), channel_id=1, source_target_pairs={{0,2},{1,3},{2,0},{3,1},{4,6},{5,7},{6,4},{7,5},{8,10},{9,11},{10,... | collective-permute-start | bytes 786440 | tf_op jit(solution)/shard_map/ppermute | solution.py:338
  16.2 11.0 %collective-permute-start.4 = (bf16[128,1024]{1,0:T(8,128)(2,1)S(1)}, bf16[128,1024]{1,0:T(8,128)(2,1)S(1)}, u32[]{:S(2)}, u32[]{:S(2)}) collective-permute-start(bf16[128,1024]{1,0:T(8,128)(2,1)S(1)} %collective-permute-done.refs_2_.refs_3_), channel_id=1, source_target_pairs={{0,4},{1,5},{2,6},{3,7},{4,8},{5,9},{6,10},{7,11},{8,12},{9,13},{1... | collective-permute-start | bytes 786440 | tf_op jit(solution)/shard_map/ppermute | solution.py:338
  17.9 9.5 %collective-permute-start.5 = (bf16[128,1024]{1,0:T(8,128)(2,1)S(1)}, bf16[128,1024]{1,0:T(8,128)(2,1)S(1)}, u32[]{:S(2)}, u32[]{:S(2)}) collective-permute-start(bf16[128,1024]{1,0:T(8,128)(2,1)S(1)} %collective-permute-done.refs_2_.refs_3_), channel_id=1, source_target_pairs={{0,2},{1,3},{2,0},{3,1},{4,6},{5,7},{6,4},{7,5},{8,10},{9,11},{10,... | collective-permute-start | bytes 786440 | tf_op jit(solution)/shard_map/ppermute | solution.py:338
  21.8 13.2 %collective-permute-start.10 = (bf16[128,1024]{1,0:T(8,128)(2,1)S(1)}, bf16[128,1024]{1,0:T(8,128)(2,1)S(1)}, u32[]{:S(2)}, u32[]{:S(2)}) collective-permute-start(bf16[128,1024]{1,0:T(8,128)(2,1)S(1)} %collective-permute-done.6.refs_2_.refs_5_), channel_id=1, source_target_pairs={{8,12},{9,13},{10,14},{11,15},{24,28},{25,29},{26,30},{27,31}} | collective-permute-start | bytes 786440 | tf_op jit(solution)/shard_map/ppermute | solution.py:338
  23.3 11.7 %collective-permute-start.11 = (bf16[128,1024]{1,0:T(8,128)(2,1)S(1)}, bf16[128,1024]{1,0:T(8,128)(2,1)S(1)}, u32[]{:S(2)}, u32[]{:S(2)}) collective-permute-start(bf16[128,1024]{1,0:T(8,128)(2,1)S(1)} %collective-permute-done.6.refs_2_.refs_5_), channel_id=1, source_target_pairs={{0,2},{1,3},{2,0},{3,1},{4,6},{5,7},{6,4},{7,5},{8,10},{9,11},{10,... | collective-permute-start | bytes 786440 | tf_op jit(solution)/shard_map/ppermute | solution.py:338
  27.4 9.8 %collective-permute-start.8 = (bf16[128,1024]{1,0:T(8,128)(2,1)S(1)}, bf16[128,1024]{1,0:T(8,128)(2,1)S(1)}, u32[]{:S(2)}, u32[]{:S(2)}) collective-permute-start(bf16[128,1024]{1,0:T(8,128)(2,1)S(1)} %collective-permute-done.4.refs_4_.refs_5_), channel_id=1, source_target_pairs={{8,12},{9,13},{10,14},{11,15},{24,28},{25,29},{26,30},{27,31}} | collective-permute-start | bytes 786440 | tf_op jit(solution)/shard_map/ppermute | solution.py:338
  28.7 9.9 %collective-permute-start.9 = (bf16[128,1024]{1,0:T(8,128)(2,1)S(1)}, bf16[128,1024]{1,0:T(8,128)(2,1)S(1)}, u32[]{:S(2)}, u32[]{:S(2)}) collective-permute-start(bf16[128,1024]{1,0:T(8,128)(2,1)S(1)} %collective-permute-done.4.refs_4_.refs_5_), channel_id=1, source_target_pairs={{0,2},{1,3},{2,0},{3,1},{4,6},{5,7},{6,4},{7,5},{8,10},{9,11},{10,... | collective-permute-start | bytes 786440 | tf_op jit(solution)/shard_map/ppermute | solution.py:338
  35.0 8.0 %collective-permute-start.13 = (bf16[128,1024]{1,0:T(8,128)(2,1)S(1)}, bf16[128,1024]{1,0:T(8,128)(2,1)S(1)}, u32[]{:S(2)}, u32[]{:S(2)}) collective-permute-start(bf16[128,1024]{1,0:T(8,128)(2,1)S(1)} %collective-permute-done.10.refs_2_.refs_7_), channel_id=1, source_target_pairs={{0,2},{1,3},{2,0},{3,1},{4,6},{5,7},{6,4},{7,5},{8,10},{9,11},{10,... | collective-permute-start | bytes 786440 | tf_op jit(solution)/shard_map/ppermute | solution.py:338
  38.6 27.9 %collective-permute-start.12 = (bf16[128,1024]{1,0:T(8,128)(2,1)S(1)}, bf16[128,1024]{1,0:T(8,128)(2,1)S(1)}, u32[]{:S(2)}, u32[]{:S(2)}) collective-permute-start(bf16[128,1024]{1,0:T(8,128)(2,1)S(1)} %collective-permute-done.9.refs_3_.refs_8_), channel_id=1, source_target_pairs={{8,12},{9,13},{10,14},{11,15},{24,28},{25,29},{26,30},{27,31}} | collective-permute-start | bytes 786440 | tf_op jit(solution)/shard_map/ppermute | solution.py:338

commit v4 on v3

--- a/solution.py
+++ b/solution.py
@@ -155,7 +155,7 @@
         w = jnp.exp2(s * FACTOR)
         if first:
             j = lax.broadcasted_iota(jnp.int32, (rows, k * lanes), 0)
-            own = jnp.where(j <= slot(t, (rows, k * lanes)), w[:rows], 0.0)
+            own = jnp.where(j <= slot(t, (1, k * lanes)), w[:rows], 0.0)
             w = jnp.concatenate([own, w[rows:]], axis=0) if n > 1 else own
         mixed = jnp.dot(v_buf[h], w.astype(jnp.bfloat16), preferred_element_type=jnp.float32)[:STATE]
         if not first:
@@ -195,7 +195,7 @@
             s = jnp.dot(key_value(i, l, h)[0], q, preferred_element_type=jnp.float32)
             allowed = j < live_keys(table_ref, me, stride, move)
             if move is None:
-                allowed = allowed & (j <= slot(t, (rows, lanes)))
+                allowed = allowed & (j <= slot(t, (1, lanes)))
             pieces.append(jnp.where(allowed, s, NEG))
         top = jnp.max(pieces[0], axis=0, keepdims=True)
         for s in pieces[1:]:

time: 91.7 us -> 91.2 us (level)
  the two profiles are of different devices: /device:TPU:26 before, /device:TPU:16 now
where the time goes in v4:
time: 91.2 us; the launch traced here: 91.5 us
  Pallas kernels  67.6 us (74%)
  starting transfers between devices  16 us (18%)
  waiting for transfers between devices  3.52 us (4%)
  local copies, waits for them, and re-layouts  3.25 us (4%)
    pallas_call x9, Pallas kernels, levels(): pl.pallas_call(partial(attend, stride, moves, fold, [[block for _, block...  67.6 us
    ppermute x14, starting transfers between devices, send(): return lax.ppermute(x, 'tp', full)  16 us
    ppermute x14, waiting for transfers between devices, send(): return lax.ppermute(x, 'tp', full)  3.52 us
    unnamed x2, local copies, waits for them, and re-layouts  2.19 us
  transfers between devices with their start and end apart: 14, of which 3 were waited for; matrix products, arithmetic and copies ran while one was open for 1% of the time, Pallas kernels for 49%

profile of v4, /device:TPU:16, one launch (start us, length us, event | category | flops | bytes accessed | tf_op | source)
XLA Modules:
  0.0 91.5 jit_solution(7012812285753398104)
XLA Ops:
  0.0 1.1 %fusion = (bf16[128,1024]{1,0:T(8,128)(2,1)S(1)}, bf16[128,1024]{1,0:T(8,128)(2,1)S(1)}) fusion(bf16[128,2048]{1,0:T(8,128)(2,1)} %param.5), kind=kLoop, calls=%fused_computation.1 | loop fusion | bytes 1048576 | tf_op jit(solution)/shard_map/slice | solution.py:358
  1.1 1.6 %collective-permute-start.2 = (bf16[128,1024]{1,0:T(8,128)(2,1)S(1)}, bf16[128,1024]{1,0:T(8,128)(2,1)S(1)}, u32[]{:S(2)}, u32[]{:S(2)}) collective-permute-start(bf16[128,1024]{1,0:T(8,128)(2,1)S(1)} %get-tuple-element.81.refs_1_.refs_2_), channel_id=1, source_target_pairs={{0,4},{1,5},{2,6},{3,7},{4,8},{5,9},{6,10},{7,11},{8,12},{9,13},{1... | collective-permute-start | bytes 786440 | tf_op jit(solution)/shard_map/ppermute | solution.py:338
  2.7 1.5 %collective-permute-start.3 = (bf16[128,1024]{1,0:T(8,128)(2,1)S(1)}, bf16[128,1024]{1,0:T(8,128)(2,1)S(1)}, u32[]{:S(2)}, u32[]{:S(2)}) collective-permute-start(bf16[128,1024]{1,0:T(8,128)(2,1)S(1)} %get-tuple-element.81.refs_1_.refs_2_), channel_id=1, source_target_pairs={{0,2},{1,3},{2,0},{3,1},{4,6},{5,7},{6,4},{7,5},{8,10},{9,11},{10,... | collective-permute-start | bytes 786440 | tf_op jit(solution)/shard_map/ppermute | solution.py:338
  5.6 2.2 %copy-done = bf16[128,16384]{1,0:T(8,128)(2,1)S(1)} copy-done((bf16[128,16384]{1,0:T(8,128)(2,1)S(1)}, bf16[128,16384]{1,0:T(8,128)(2,1)}, u32[]{:S(2)}) %copy-start) | copy-done | bytes 4194328
  7.7 2.6 %levels_1_first.2 = (bf16[4,128,2048]{2,1,0:T(8,128)(2,1)S(1)}, f32[4,136,2048]{2,1,0:T(8,128)S(1)}) custom-call(s32[33]{0:T(128)S(1)} %pad_add_fusion.table_ref, bf16[128,16384]{1,0:T(8,128)(2,1)S(1)} %copy-done, bf16[128,1024]{1,0:T(8,128)(2,1)S(1)} %get-tuple-element.81.refs_1_.refs_2_), custom_call_target="tpu_custom_call" | custom-call | flops 536870912 | bytes 2097152 | tf_op jit(solution)/shard_map/levels_1_first/pallas_call | solution.py:296
  10.4 1.5 %collective-permute-done.3.refs_3_.refs_4_ = bf16[128,1024]{1,0:T(8,128)(2,1)S(1)} collective-permute-done((bf16[128,1024]{1,0:T(8,128)(2,1)S(1)}, bf16[128,1024]{1,0:T(8,128)(2,1)S(1)}, u32[]{:S(2)}, u32[]{:S(2)}) %collective-permute-start.3) | collective-permute-done | bytes 262176 | tf_op jit(solution)/shard_map/ppermute | solution.py:338
  12.0 1.7 %collective-permute-start.7 = (bf16[128,1024]{1,0:T(8,128)(2,1)S(1)}, bf16[128,1024]{1,0:T(8,128)(2,1)S(1)}, u32[]{:S(2)}, u32[]{:S(2)}) collective-permute-start(bf16[128,1024]{1,0:T(8,128)(2,1)S(1)} %collective-permute-done.2.refs_2_.refs_3_), channel_id=1, source_target_pairs={{0,2},{1,3},{2,0},{3,1},{4,6},{5,7},{6,4},{7,5},{8,10},{9,11},{10,... | collective-permute-start | bytes 786440 | tf_op jit(solution)/shard_map/ppermute | solution.py:338
  13.7 2.6 %levels_1_first.3 = (bf16[4,128,2048]{2,1,0:T(8,128)(2,1)S(1)}, f32[4,136,2048]{2,1,0:T(8,128)S(1)}) custom-call(s32[33]{0:T(128)S(1)} %pad_add_fusion.table_ref, bf16[128,16384]{1,0:T(8,128)(2,1)S(1)} %copy-done, bf16[128,1024]{1,0:T(8,128)(2,1)S(1)} %get-tuple-element.82.refs_1_.refs_2_), custom_call_target="tpu_custom_call" | custom-call | flops 536870912 | bytes 2097152 | tf_op jit(solution)/shard_map/levels_1_first/pallas_call | solution.py:296
  16.3 1.2 %collective-permute-done.1.refs_3_.refs_4_ = bf16[128,1024]{1,0:T(8,128)(2,1)S(1)} collective-permute-done((bf16[128,1024]{1,0:T(8,128)(2,1)S(1)}, bf16[128,1024]{1,0:T(8,128)(2,1)S(1)}, u32[]{:S(2)}, u32[]{:S(2)}) %collective-permute-start.1) | collective-permute-done | bytes 262176 | tf_op jit(solution)/shard_map/ppermute | solution.py:338
  17.6 1.7 %collective-permute-start.5 = (bf16[128,1024]{1,0:T(8,128)(2,1)S(1)}, bf16[128,1024]{1,0:T(8,128)(2,1)S(1)}, u32[]{:S(2)}, u32[]{:S(2)}) collective-permute-start(bf16[128,1024]{1,0:T(8,128)(2,1)S(1)} %collective-permute-done.refs_2_.refs_3_), channel_id=1, source_target_pairs={{0,2},{1,3},{2,0},{3,1},{4,6},{5,7},{6,4},{7,5},{8,10},{9,11},{10,... | collective-permute-start | bytes 786440 | tf_op jit(solution)/shard_map/ppermute | solution.py:338
  19.2 3.1 %levels_2.4.refs_1_ = f32[4,136,2048]{2,1,0:T(8,128)S(1)} custom-call(s32[33]{0:T(128)S(1)} %pad_add_fusion.table_ref, bf16[4,128,2048]{2,1,0:T(8,128)(2,1)S(1)} %get-tuple-element.79.refs_0_, f32[4,136,2048]{2,1,0:T(8,128)S(1)} %get-tuple-element.52.refs_1_, bf16[128,1024]{1,0:T(8,128)(2,1)S(1)} %collective-permute-done.2.refs_2_.refs_3_, ...), custom_call_target="tpu_custom_call" | custom-call | flops 1073741824 | bytes 2097152 | tf_op jit(solution)/shard_map/levels_2/pallas_call | solution.py:296
  22.4 0.8 collective-permute-done.7.refs_3_.refs_6_
  23.2 2.1 %collective-permute-start.10 = (bf16[128,1024]{1,0:T(8,128)(2,1)S(1)}, bf16[128,1024]{1,0:T(8,128)(2,1)S(1)}, u32[]{:S(2)}, u32[]{:S(2)}) collective-permute-start(bf16[128,1024]{1,0:T(8,128)(2,1)S(1)} %collective-permute-done.6.refs_2_.refs_5_), channel_id=1, source_target_pairs={{8,12},{9,13},{10,14},{11,15},{24,28},{25,29},{26,30},{27,31}} | collective-permute-start | bytes 786440 | tf_op jit(solution)/shard_map/ppermute | solution.py:338
  25.3 1.7 %collective-permute-start.11 = (bf16[128,1024]{1,0:T(8,128)(2,1)S(1)}, bf16[128,1024]{1,0:T(8,128)(2,1)S(1)}, u32[]{:S(2)}, u32[]{:S(2)}) collective-permute-start(bf16[128,1024]{1,0:T(8,128)(2,1)S(1)} %collective-permute-done.6.refs_2_.refs_5_), channel_id=1, source_target_pairs={{0,2},{1,3},{2,0},{3,1},{4,6},{5,7},{6,4},{7,5},{8,10},{9,11},{10,... | collective-permute-start | bytes 786440 | tf_op jit(solution)/shard_map/ppermute | solution.py:338
  27.0 3.1 %levels_2.5.refs_1_ = f32[4,136,2048]{2,1,0:T(8,128)S(1)} custom-call(s32[33]{0:T(128)S(1)} %pad_add_fusion.table_ref, bf16[4,128,2048]{2,1,0:T(8,128)(2,1)S(1)} %get-tuple-element.79.refs_0_, f32[4,136,2048]{2,1,0:T(8,128)S(1)} %levels_2.4.refs_1_, bf16[128,1024]{1,0:T(8,128)(2,1)S(1)} %collective-permute-done.6.refs_2_.refs_5_, ...), custom_call_target="tpu_custom_call" | custom-call | flops 1073741824 | bytes 2097152 | tf_op jit(solution)/shard_map/levels_2/pallas_call | solution.py:296
  30.2 1.3 %collective-permute-start.8 = (bf16[128,1024]{1,0:T(8,128)(2,1)S(1)}, bf16[128,1024]{1,0:T(8,128)(2,1)S(1)}, u32[]{:S(2)}, u32[]{:S(2)}) collective-permute-start(bf16[128,1024]{1,0:T(8,128)(2,1)S(1)} %collective-permute-done.4.refs_4_.refs_5_), channel_id=1, source_target_pairs={{8,12},{9,13},{10,14},{11,15},{24,28},{25,29},{26,30},{27,31}} | collective-permute-start | bytes 786440 | tf_op jit(solution)/shard_map/ppermute | solution.py:338
  31.5 1.0 %collective-permute-start.9 = (bf16[128,1024]{1,0:T(8,128)(2,1)S(1)}, bf16[128,1024]{1,0:T(8,128)(2,1)S(1)}, u32[]{:S(2)}, u32[]{:S(2)}) collective-permute-start(bf16[128,1024]{1,0:T(8,128)(2,1)S(1)} %collective-permute-done.4.refs_4_.refs_5_), channel_id=1, source_target_pairs={{0,2},{1,3},{2,0},{3,1},{4,6},{5,7},{6,4},{7,5},{8,10},{9,11},{10,... | collective-permute-start | bytes 786440 | tf_op jit(solution)/shard_map/ppermute | solution.py:338
  32.5 5.1 %levels_4.1.refs_1_ = f32[4,136,2048]{2,1,0:T(8,128)S(1)} custom-call(s32[33]{0:T(128)S(1)} %pad_add_fusion.table_ref, bf16[4,128,2048]{2,1,0:T(8,128)(2,1)S(1)} %get-tuple-element.75.refs_0_, f32[4,136,2048]{2,1,0:T(8,128)S(1)} %get-tuple-element.66.refs_1_, bf16[128,1024]{1,0:T(8,128)(2,1)S(1)} %collective-permute-done.refs_2_.refs_3_, ...), custom_call_target="tpu_custom_call" | custom-call | flops 2147483648 | bytes 2097152 | tf_op jit(solution)/shard_map/levels_4/pallas_call | solution.py:296
  37.6 1.2 %collective-permute-start.13 = (bf16[128,1024]{1,0:T(8,128)(2,1)S(1)}, bf16[128,1024]{1,0:T(8,128)(2,1)S(1)}, u32[]{:S(2)}, u32[]{:S(2)}) collective-permute-start(bf16[128,1024]{1,0:T(8,128)(2,1)S(1)} %collective-permute-done.10.refs_2_.refs_7_), channel_id=1, source_target_pairs={{0,2},{1,3},{2,0},{3,1},{4,6},{5,7},{6,4},{7,5},{8,10},{9,11},{10,... | collective-permute-start | bytes 786440 | tf_op jit(solution)/shard_map/ppermute | solution.py:338
  38.8 3.1 %levels_2.6.refs_1_ = f32[4,136,2048]{2,1,0:T(8,128)S(1)} custom-call(s32[33]{0:T(128)S(1)} %pad_add_fusion.table_ref, bf16[4,128,2048]{2,1,0:T(8,128)(2,1)S(1)} %get-tuple-element.79.refs_0_, f32[4,136,2048]{2,1,0:T(8,128)S(1)} %levels_2.5.refs_1_, bf16[128,1024]{1,0:T(8,128)(2,1)S(1)} %collective-permute-done.10.refs_2_.refs_7_, ...), custom_call_target="tpu_custom_call" | custom-call | flops 1073741824 | bytes 2097152 | tf_op jit(solution)/shard_map/levels_2/pallas_call | solution.py:296
  41.9 1.5 %collective-permute-start.12 = (bf16[128,1024]{1,0:T(8,128)(2,1)S(1)}, bf16[128,1024]{1,0:T(8,128)(2,1)S(1)}, u32[]{:S(2)}, u32[]{:S(2)}) collective-permute-start(bf16[128,1024]{1,0:T(8,128)(2,1)S(1)} %collective-permute-done.9.refs_3_.refs_8_), channel_id=1, source_target_pairs={{8,12},{9,13},{10,14},{11,15},{24,28},{25,29},{26,30},{27,31}} | collective-permute-start | bytes 786440 | tf_op jit(solution)/shard_map/ppermute | solution.py:338
  43.5 3.1 %levels_2.7.refs_1_ = f32[4,136,2048]{2,1,0:T(8,128)S(1)} custom-call(s32[33]{0:T(128)S(1)} %pad_add_fusion.table_ref, bf16[4,128,2048]{2,1,0:T(8,128)(2,1)S(1)} %get-tuple-element.75.refs_0_, f32[4,136,2048]{2,1,0:T(8,128)S(1)} %levels_4.1.refs_1_, bf16[128,1024]{1,0:T(8,128)(2,1)S(1)} %collective-permute-done.8.refs_2_.refs_7_, ...), custom_call_target="tpu_custom_call" | custom-call | flops 1073741824 | bytes 2097152 | tf_op jit(solution)/shard_map/levels_2/pallas_call | solution.py:296
  46.6 22.2 %levels_1_last.2.refs_10_ = bf16[128,16384]{1,0:T(8,128)(2,1)} custom-call(s32[33]{0:T(128)S(1)} %pad_add_fusion.table_ref, bf16[4,128,2048]{2,1,0:T(8,128)(2,1)S(1)} %get-tuple-element.79.refs_0_, f32[4,136,2048]{2,1,0:T(8,128)S(1)} %levels_2.6.refs_1_, bf16[128,1024]{1,0:T(8,128)(2,1)S(1)} %get-tuple-element.81.refs_1_.refs_2_, ...), custom_call_target="tpu_custom_call" | custom-call | flops 536870912 | bytes 2097152 | tf_op jit(solution)/shard_map/levels_1_last/pallas_call | solution.py:296
  68.8 22.5 %levels_1_last.3 = bf16[128,16384]{1,0:T(8,128)(2,1)} custom-call(s32[33]{0:T(128)S(1)} %pad_add_fusion.table_ref, bf16[4,128,2048]{2,1,0:T(8,128)(2,1)S(1)} %get-tuple-element.75.refs_0_, f32[4,136,2048]{2,1,0:T(8,128)S(1)} %levels_2.7.refs_1_, bf16[128,1024]{1,0:T(8,128)(2,1)S(1)} %get-tuple-element.82.refs_1_.refs_2_, ...), custom_call_target="tpu_custom_call", output_to_operand_aliasing={{}: (11, {})} | custom-call | flops 536870912 | bytes 2097152 | tf_op jit(solution)/shard_map/levels_1_last/pallas_call | solution.py:296
  (17 shorter events, 1.5 us)
Async XLA Ops:
  1.1 9.3 %collective-permute-start.2 = (bf16[128,1024]{1,0:T(8,128)(2,1)S(1)}, bf16[128,1024]{1,0:T(8,128)(2,1)S(1)}, u32[]{:S(2)}, u32[]{:S(2)}) collective-permute-start(bf16[128,1024]{1,0:T(8,128)(2,1)S(1)} %get-tuple-element.81.refs_1_.refs_2_), channel_id=1, source_target_pairs={{0,4},{1,5},{2,6},{3,7},{4,8},{5,9},{6,10},{7,11},{8,12},{9,13},{1... | collective-permute-start | bytes 786440 | tf_op jit(solution)/shard_map/ppermute | solution.py:338
  2.7 9.2 %collective-permute-start.3 = (bf16[128,1024]{1,0:T(8,128)(2,1)S(1)}, bf16[128,1024]{1,0:T(8,128)(2,1)S(1)}, u32[]{:S(2)}, u32[]{:S(2)}) collective-permute-start(bf16[128,1024]{1,0:T(8,128)(2,1)S(1)} %get-tuple-element.81.refs_1_.refs_2_), channel_id=1, source_target_pairs={{0,2},{1,3},{2,0},{3,1},{4,6},{5,7},{6,4},{7,5},{8,10},{9,11},{10,... | collective-permute-start | bytes 786440 | tf_op jit(solution)/shard_map/ppermute | solution.py:338
  4.2 12.1 %collective-permute-start = (bf16[128,1024]{1,0:T(8,128)(2,1)S(1)}, bf16[128,1024]{1,0:T(8,128)(2,1)S(1)}, u32[]{:S(2)}, u32[]{:S(2)}) collective-permute-start(bf16[128,1024]{1,0:T(8,128)(2,1)S(1)} %get-tuple-element.82.refs_1_.refs_2_), channel_id=1, source_target_pairs={{0,4},{1,5},{2,6},{3,7},{4,8},{5,9},{6,10},{7,11},{8,12},{9,13},{1... | collective-permute-start | bytes 786440 | tf_op jit(solution)/shard_map/ppermute | solution.py:338
  4.4 13.1 %collective-permute-start.1 = (bf16[128,1024]{1,0:T(8,128)(2,1)S(1)}, bf16[128,1024]{1,0:T(8,128)(2,1)S(1)}, u32[]{:S(2)}, u32[]{:S(2)}) collective-permute-start(bf16[128,1024]{1,0:T(8,128)(2,1)S(1)} %get-tuple-element.82.refs_1_.refs_2_), channel_id=1, source_target_pairs={{0,2},{1,3},{2,0},{3,1},{4,6},{5,7},{6,4},{7,5},{8,10},{9,11},{10,... | collective-permute-start | bytes 786440 | tf_op jit(solution)/shard_map/ppermute | solution.py:338
  5.5 2.2 %copy-start = (bf16[128,16384]{1,0:T(8,128)(2,1)S(1)}, bf16[128,16384]{1,0:T(8,128)(2,1)}, u32[]{:S(2)}) copy-start(bf16[128,16384]{1,0:T(8,128)(2,1)} %refs_0_.3) | copy-start | bytes 12582916
  11.9 10.5 %collective-permute-start.6 = (bf16[128,1024]{1,0:T(8,128)(2,1)S(1)}, bf16[128,1024]{1,0:T(8,128)(2,1)S(1)}, u32[]{:S(2)}, u32[]{:S(2)}) collective-permute-start(bf16[128,1024]{1,0:T(8,128)(2,1)S(1)} %collective-permute-done.2.refs_2_.refs_3_), channel_id=1, source_target_pairs={{0,4},{1,5},{2,6},{3,7},{4,8},{5,9},{6,10},{7,11},{8,12},{9,13},{1... | collective-permute-start | bytes 786440 | tf_op jit(solution)/shard_map/ppermute | solution.py:338
  12.0 11.2 %collective-permute-start.7 = (bf16[128,1024]{1,0:T(8,128)(2,1)S(1)}, bf16[128,1024]{1,0:T(8,128)(2,1)S(1)}, u32[]{:S(2)}, u32[]{:S(2)}) collective-permute-start(bf16[128,1024]{1,0:T(8,128)(2,1)S(1)} %collective-permute-done.2.refs_2_.refs_3_), channel_id=1, source_target_pairs={{0,2},{1,3},{2,0},{3,1},{4,6},{5,7},{6,4},{7,5},{8,10},{9,11},{10,... | collective-permute-start | bytes 786440 | tf_op jit(solution)/shard_map/ppermute | solution.py:338
  17.5 12.6 %collective-permute-start.4 = (bf16[128,1024]{1,0:T(8,128)(2,1)S(1)}, bf16[128,1024]{1,0:T(8,128)(2,1)S(1)}, u32[]{:S(2)}, u32[]{:S(2)}) collective-permute-start(bf16[128,1024]{1,0:T(8,128)(2,1)S(1)} %collective-permute-done.refs_2_.refs_3_), channel_id=1, source_target_pairs={{0,4},{1,5},{2,6},{3,7},{4,8},{5,9},{6,10},{7,11},{8,12},{9,13},{1... | collective-permute-start | bytes 786440 | tf_op jit(solution)/shard_map/ppermute | solution.py:338
  17.6 12.6 %collective-permute-start.5 = (bf16[128,1024]{1,0:T(8,128)(2,1)S(1)}, bf16[128,1024]{1,0:T(8,128)(2,1)S(1)}, u32[]{:S(2)}, u32[]{:S(2)}) collective-permute-start(bf16[128,1024]{1,0:T(8,128)(2,1)S(1)} %collective-permute-done.refs_2_.refs_3_), channel_id=1, source_target_pairs={{0,2},{1,3},{2,0},{3,1},{4,6},{5,7},{6,4},{7,5},{8,10},{9,11},{10,... | collective-permute-start | bytes 786440 | tf_op jit(solution)/shard_map/ppermute | solution.py:338
  23.2 14.4 %collective-permute-start.10 = (bf16[128,1024]{1,0:T(8,128)(2,1)S(1)}, bf16[128,1024]{1,0:T(8,128)(2,1)S(1)}, u32[]{:S(2)}, u32[]{:S(2)}) collective-permute-start(bf16[128,1024]{1,0:T(8,128)(2,1)S(1)} %collective-permute-done.6.refs_2_.refs_5_), channel_id=1, source_target_pairs={{8,12},{9,13},{10,14},{11,15},{24,28},{25,29},{26,30},{27,31}} | collective-permute-start | bytes 786440 | tf_op jit(solution)/shard_map/ppermute | solution.py:338
  25.3 12.3 %collective-permute-start.11 = (bf16[128,1024]{1,0:T(8,128)(2,1)S(1)}, bf16[128,1024]{1,0:T(8,128)(2,1)S(1)}, u32[]{:S(2)}, u32[]{:S(2)}) collective-permute-start(bf16[128,1024]{1,0:T(8,128)(2,1)S(1)} %collective-permute-done.6.refs_2_.refs_5_), channel_id=1, source_target_pairs={{0,2},{1,3},{2,0},{3,1},{4,6},{5,7},{6,4},{7,5},{8,10},{9,11},{10,... | collective-permute-start | bytes 786440 | tf_op jit(solution)/shard_map/ppermute | solution.py:338
  30.2 11.7 %collective-permute-start.8 = (bf16[128,1024]{1,0:T(8,128)(2,1)S(1)}, bf16[128,1024]{1,0:T(8,128)(2,1)S(1)}, u32[]{:S(2)}, u32[]{:S(2)}) collective-permute-start(bf16[128,1024]{1,0:T(8,128)(2,1)S(1)} %collective-permute-done.4.refs_4_.refs_5_), channel_id=1, source_target_pairs={{8,12},{9,13},{10,14},{11,15},{24,28},{25,29},{26,30},{27,31}} | collective-permute-start | bytes 786440 | tf_op jit(solution)/shard_map/ppermute | solution.py:338
  31.5 10.4 %collective-permute-start.9 = (bf16[128,1024]{1,0:T(8,128)(2,1)S(1)}, bf16[128,1024]{1,0:T(8,128)(2,1)S(1)}, u32[]{:S(2)}, u32[]{:S(2)}) collective-permute-start(bf16[128,1024]{1,0:T(8,128)(2,1)S(1)} %collective-permute-done.4.refs_4_.refs_5_), channel_id=1, source_target_pairs={{0,2},{1,3},{2,0},{3,1},{4,6},{5,7},{6,4},{7,5},{8,10},{9,11},{10,... | collective-permute-start | bytes 786440 | tf_op jit(solution)/shard_map/ppermute | solution.py:338
  37.6 9.0 %collective-permute-start.13 = (bf16[128,1024]{1,0:T(8,128)(2,1)S(1)}, bf16[128,1024]{1,0:T(8,128)(2,1)S(1)}, u32[]{:S(2)}, u32[]{:S(2)}) collective-permute-start(bf16[128,1024]{1,0:T(8,128)(2,1)S(1)} %collective-permute-done.10.refs_2_.refs_7_), channel_id=1, source_target_pairs={{0,2},{1,3},{2,0},{3,1},{4,6},{5,7},{6,4},{7,5},{8,10},{9,11},{10,... | collective-permute-start | bytes 786440 | tf_op jit(solution)/shard_map/ppermute | solution.py:338
  41.9 26.9 %collective-permute-start.12 = (bf16[128,1024]{1,0:T(8,128)(2,1)S(1)}, bf16[128,1024]{1,0:T(8,128)(2,1)S(1)}, u32[]{:S(2)}, u32[]{:S(2)}) collective-permute-start(bf16[128,1024]{1,0:T(8,128)(2,1)S(1)} %collective-permute-done.9.refs_3_.refs_8_), channel_id=1, source_target_pairs={{8,12},{9,13},{10,14},{11,15},{24,28},{25,29},{26,30},{27,31}} | collective-permute-start | bytes 786440 | tf_op jit(solution)/shard_map/ppermute | solution.py:338
